TPU v7x, 128 devices: a whole 4x4x4 slice. The times are simulated.
128 devices in a mesh: gx: 16 (over x, y_hi, core), gy: 8 (over z, y_lo).
Axes of the slice: x: 4, y: 4 (y_hi: 2, y_lo: 2; y = y_hi * 2 + y_lo), z: 4, core: 2. Of those that a mesh axis runs over, the one named last changes fastest.
Arguments:
- features: bfloat16 [96, 32, 64, 128], P(None, 'gx', 'gy'), may hold values from -6 to 6
- cotangent: bfloat16 [96, 32, 64, 128], P(None, 'gx', 'gy'), may hold values from -6 to 6
- weights: bfloat16 [27, 96, 96], replicated, may hold values from -0.125 to 0.125
- ground: int32 [32, 64], P('gx', 'gy'), may hold values from 0 to 31
- thick: int32 [32, 64], P('gx', 'gy'), may hold values from 48 to 96
Outputs:
- outputs: bfloat16 [96, 32, 64, 128], P(None, 'gx', 'gy')
- input_grad: bfloat16 [96, 32, 64, 128], P(None, 'gx', 'gy')
- weight_grad: float32 [27, 96, 96], replicated
All inputs are finite; a program needn't handle non-finite values.
Results may differ from a plain program's by a relative error of at most 0.001.
Values may be sent and summed in bfloat16 or wider, within the bound.
A program may use at most 128 MiB of HBM per device.

v0:
```python
import math

import jax
import jax.numpy as jnp
from jax import lax
from jax.sharding import PartitionSpec as P


def with_halo(cells, sides, width):
    for axis, dim in sides:
        count = lax.axis_size(axis)
        ends = count - 1
        head = lax.slice_in_dim(cells, 0, width, axis=dim)
        tail = lax.slice_in_dim(cells, cells.shape[dim] - width, cells.shape[dim], axis=dim)
        cells = jnp.concatenate(
            [
                lax.ppermute(tail, axis, [(i, (i + 1) % count) for i in range(ends)]),
                cells,
                lax.ppermute(head, axis, [((i + 1) % count, i) for i in range(ends)]),
            ],
            axis=dim,
        )
    return cells


def widen(field):
    return with_halo(field, (("gx", 1), ("gy", 2)), 1)


def shards(features, cotangent, weights, ground, thick):
    channels, width_x, width_y, depth_z = features.shape
    heights = lax.broadcasted_iota(jnp.int32, (width_x, width_y, depth_z), 2)
    ceiling = (ground + thick)[:, :, None]
    occupied = ((heights >= ground[:, :, None]) & (heights < ceiling)).astype(jnp.bfloat16)
    masked_in = features * occupied[None]
    masked_cot = cotangent * occupied[None]
    wide_in = widen(masked_in)
    wide_cot = widen(masked_cot)
    depth_pad = ((0, 0), (0, 0), (0, 0), (1, 1))
    padded_in = jnp.pad(wide_in, depth_pad)
    padded_cot = jnp.pad(wide_cot, depth_pad)
    voxels = width_x * width_y * depth_z
    cot_flat = masked_cot.reshape(channels, voxels)
    forward_sum = jnp.zeros((channels, voxels), jnp.float32)
    backward_sum = jnp.zeros((channels, voxels), jnp.float32)
    grad_blocks = []
    for slab_x in range(3):
        plane_offset = slab_x - 1
        forward_stack = jnp.concatenate(
            [
                padded_in[
                    :,
                    1 + plane_offset : 1 + plane_offset + width_x,
                    lane_y : lane_y + width_y,
                    lane_z : lane_z + depth_z,
                ].reshape(channels, voxels)
                for lane_y in range(3)
                for lane_z in range(3)
            ],
            0,
        )
        backward_stack = jnp.concatenate(
            [
                padded_cot[
                    :,
                    1 - plane_offset : 1 - plane_offset + width_x,
                    2 - lane_y : 2 - lane_y + width_y,
                    2 - lane_z : 2 - lane_z + depth_z,
                ].reshape(channels, voxels)
                for lane_y in range(3)
                for lane_z in range(3)
            ],
            0,
        )
        weight_block = weights[slab_x * 9 : (slab_x + 1) * 9]
        forward_matrix = jnp.transpose(weight_block, (1, 0, 2)).reshape(channels, 9 * channels)
        backward_matrix = jnp.transpose(weight_block, (2, 0, 1)).reshape(channels, 9 * channels)
        forward_sum = forward_sum + jnp.dot(
            forward_matrix, forward_stack, preferred_element_type=jnp.float32
        )
        backward_sum = backward_sum + jnp.dot(
            backward_matrix, backward_stack, preferred_element_type=jnp.float32
        )
        local_grad = lax.dot_general(
            cot_flat, forward_stack, (((1,), (1,)), ((), ())), preferred_element_type=jnp.float32
        )
        local_grad = jnp.transpose(local_grad.reshape(channels, 9, channels), (1, 0, 2))
        grad_blocks.append(local_grad)
    weight_grad = jnp.concatenate(grad_blocks, 0)
    weight_grad = lax.psum(weight_grad, ("gx", "gy"))
    grad_scale = 1.0 / math.sqrt(voxels * lax.axis_size("gx") * lax.axis_size("gy"))
    weight_grad = weight_grad * grad_scale
    occupied_flat = occupied.reshape(1, voxels)
    outputs = (
        (forward_sum * occupied_flat)
        .astype(jnp.bfloat16)
        .reshape(channels, width_x, width_y, depth_z)
    )
    input_grad = (
        (backward_sum * occupied_flat)
        .astype(jnp.bfloat16)
        .reshape(channels, width_x, width_y, depth_z)
    )
    return (outputs, input_grad, weight_grad)


def solution(mesh):
    placed = (
        P(None, "gx", "gy", None),
        P(None, "gx", "gy", None),
        P(),
        P("gx", "gy"),
        P("gx", "gy"),
    )
    return jax.shard_map(
        shards,
        mesh=mesh,
        in_specs=placed,
        out_specs=(P(None, "gx", "gy", None), P(None, "gx", "gy", None), P()),
        check_vma=False,
    )
```

profile of v0, /device:TPU:1, one launch (start us, length us, event | category | flops | bytes accessed | tf_op | source)
XLA Modules:
  0.0 252.8 jit_solution(10022787887969348021)
XLA Ops:
  10.8 6.2 %collective-permute-start.4 = (bf16[96,1,8,128]{3,0,2,1:T(8,128)(2,1)}, bf16[96,1,8,128]{3,0,2,1:T(8,128)(2,1)S(1)}, u32[]{:S(2)}, u32[]{:S(2)}) collective-permute-start(bf16[96,1,8,128]{3,0,2,1:T(8,128)(2,1)} %get-tuple-element.67), channel_id=1, source_target_pairs={{0,8},{8,16},{16,24},{24,32},{32,40},{40,48},{48,56},{56,64},{64,7... | collective-permute-start | bytes 589832 | tf_op jit(solution)/shard_map/ppermute | solution.py:17
  17.0 1.9 collective-permute-start.5
  19.7 5.1 %collective-permute-start = (bf16[96,1,8,128]{3,0,2,1:T(8,128)(2,1)}, bf16[96,1,8,128]{3,0,2,1:T(8,128)(2,1)S(1)}, u32[]{:S(2)}, u32[]{:S(2)}) collective-permute-start(bf16[96,1,8,128]{3,0,2,1:T(8,128)(2,1)} %get-tuple-element.71), channel_id=1, source_target_pairs={{0,8},{8,16},{16,24},{24,32},{32,40},{40,48},{48,56},{56,64},{64,7... | collective-permute-start | bytes 589832 | tf_op jit(solution)/shard_map/ppermute | solution.py:17
  24.8 1.9 collective-permute-start.1
  31.3 2.3 collective-permute-start.6
  33.6 1.3 collective-permute-start.7
  35.0 5.0 %collective-permute-start.2 = (bf16[96,4,1,128]{3,0,2,1:T(8,128)(2,1)S(1)}, bf16[96,4,1,128]{3,0,2,1:T(8,128)(2,1)S(1)}, u32[]{:S(2)}, u32[]{:S(2)}) collective-permute-start(bf16[96,4,1,128]{3,0,2,1:T(8,128)(2,1)S(1)} %get-tuple-element.57), channel_id=1, source_target_pairs={{0,1},{1,2},{2,3},{3,4},{4,5},{5,6},{6,7},{8,9},{9,10},{10,11},{11... | collective-permute-start | bytes 294920 | tf_op jit(solution)/shard_map/ppermute | solution.py:17
  43.5 2.7 %collective-permute-done.3 = bf16[96,4,1,128]{3,0,2,1:T(8,128)(2,1)S(1)} collective-permute-done((bf16[96,4,1,128]{3,0,2,1:T(8,128)(2,1)S(1)}, bf16[96,4,1,128]{3,0,2,1:T(8,128)(2,1)S(1)}, u32[]{:S(2)}, u32[]{:S(2)}) %collective-permute-start.3) | collective-permute-done | bytes 98336 | tf_op jit(solution)/shard_map/ppermute | solution.py:19
  53.6 1.8 select_maximum_fusion
  55.4 1.9 fusion.14
  74.0 1.8 select_maximum_fusion.4
  75.8 2.0 fusion.15
  81.6 1.7 fusion.23
  83.3 1.4 convolution_bitcast_fusion.2
  85.4 1.4 convolution_bitcast_fusion.1
  87.8 1.4 convolution_bitcast_fusion
  90.4 1.9 bitcast_dynamic-update-slice_fusion.25
  92.4 1.8 bitcast_dynamic-update-slice_fusion.24
  94.2 1.8 bitcast_dynamic-update-slice_fusion.23
  96.0 1.9 bitcast_dynamic-update-slice_fusion.22
  97.9 1.8 bitcast_dynamic-update-slice_fusion.21
  102.3 3.0 %fusion.24 = f32[2048,96]{0,1:T(8,128)S(1)} fusion(bf16[864,2048]{1,0:T(8,128)(2,1)} %bitcast_dynamic-update-slice_fusion.18, bf16[96,864]{0,1:T(8,128)(2,1)S(1)} %bitcast.338), kind=kOutput, calls=%fused_computation.117 | convolution fusion | flops 339738624 | bytes 4491264 | tf_op jit(solution)/shard_map/dot_general | solution.py:81
  115.1 128.3 %all-reduce.4.cloned.1.call-done = f32[27,96,96]{2,1,0:T(8,128)} async-done(((f32[27,96,96]{2,1,0:T(8,128)}), f32[27,96,96]{2,1,0:T(8,128)}) %all-reduce.4.cloned.1.call-update) | async-done | bytes 995344 | tf_op jit(solution)/shard_map/psum | solution.py:90
  243.4 2.5 broadcast_multiply_fusion
  (204 shorter events, 54.9 us)
Async XLA Ops:
  7.2 19.6 %copy-start.32 = (bf16[27,96,96]{2,1,0:T(8,128)(2,1)S(1)}, bf16[27,96,96]{2,1,0:T(8,128)(2,1)}, u32[]{:S(2)}) copy-start(bf16[27,96,96]{2,1,0:T(8,128)(2,1)} %param.7) | copy-start | bytes 1492996
  7.2 236.3 %all-reduce.4.cloned.1.call-start = ((), (), s32[]{:S(2)}) async-start(), calls=%async_computation | async-start | bytes 2654208 | tf_op jit(solution)/shard_map/psum | solution.py:90
  10.8 20.5 %collective-permute-start.4 = (bf16[96,1,8,128]{3,0,2,1:T(8,128)(2,1)}, bf16[96,1,8,128]{3,0,2,1:T(8,128)(2,1)S(1)}, u32[]{:S(2)}, u32[]{:S(2)}) collective-permute-start(bf16[96,1,8,128]{3,0,2,1:T(8,128)(2,1)} %get-tuple-element.67), channel_id=1, source_target_pairs={{0,8},{8,16},{16,24},{24,32},{32,40},{40,48},{48,56},{56,64},{64,7... | collective-permute-start | bytes 589832 | tf_op jit(solution)/shard_map/ppermute | solution.py:17
  17.0 14.3 %collective-permute-start.5 = (bf16[96,1,8,128]{3,0,2,1:T(8,128)(2,1)}, bf16[96,1,8,128]{3,0,2,1:T(8,128)(2,1)S(1)}, u32[]{:S(2)}, u32[]{:S(2)}) collective-permute-start(bf16[96,1,8,128]{3,0,2,1:T(8,128)(2,1)} %get-tuple-element.68), channel_id=1, source_target_pairs={{8,0},{16,8},{24,16},{32,24},{40,32},{48,40},{56,48},{64,56},{72,6... | collective-permute-start | bytes 589832 | tf_op jit(solution)/shard_map/ppermute | solution.py:19
  19.7 15.2 %collective-permute-start = (bf16[96,1,8,128]{3,0,2,1:T(8,128)(2,1)}, bf16[96,1,8,128]{3,0,2,1:T(8,128)(2,1)S(1)}, u32[]{:S(2)}, u32[]{:S(2)}) collective-permute-start(bf16[96,1,8,128]{3,0,2,1:T(8,128)(2,1)} %get-tuple-element.71), channel_id=1, source_target_pairs={{0,8},{8,16},{16,24},{24,32},{32,40},{40,48},{48,56},{56,64},{64,7... | collective-permute-start | bytes 589832 | tf_op jit(solution)/shard_map/ppermute | solution.py:17
  24.8 10.1 %collective-permute-start.1 = (bf16[96,1,8,128]{3,0,2,1:T(8,128)(2,1)}, bf16[96,1,8,128]{3,0,2,1:T(8,128)(2,1)S(1)}, u32[]{:S(2)}, u32[]{:S(2)}) collective-permute-start(bf16[96,1,8,128]{3,0,2,1:T(8,128)(2,1)} %get-tuple-element.72), channel_id=1, source_target_pairs={{8,0},{16,8},{24,16},{32,24},{40,32},{48,40},{56,48},{64,56},{72,6... | collective-permute-start | bytes 589832 | tf_op jit(solution)/shard_map/ppermute | solution.py:19
  28.0 13.5 %copy-start.7 = (bf16[96,2,8,128]{3,2,1,0:T(8,128)(2,1)}, bf16[96,2,8,128]{3,2,1,0:T(8,128)(2,1)S(1)}, u32[]{:S(2)}) copy-start(bf16[96,2,8,128]{3,2,1,0:T(8,128)(2,1)S(1)} %copy.61) | copy-start | bytes 1179652
  28.3 57.1 %copy-start.4 = (bf16[96,2048,1]{1,0,2:T(8,128)(2,1)}, bf16[96,2048,1]{1,0,2:T(8,128)(2,1)S(1)}, u32[]{:S(2)}) copy-start(bf16[96,2048,1]{1,0,2:T(8,128)(2,1)S(1)} %reshape.308) | copy-start | bytes 1179652
  31.3 16.4 %collective-permute-start.6 = (bf16[96,4,1,128]{3,0,2,1:T(8,128)(2,1)S(1)}, bf16[96,4,1,128]{3,0,2,1:T(8,128)(2,1)S(1)}, u32[]{:S(2)}, u32[]{:S(2)}) collective-permute-start(bf16[96,4,1,128]{3,0,2,1:T(8,128)(2,1)S(1)} %get-tuple-element.53), channel_id=1, source_target_pairs={{0,1},{1,2},{2,3},{3,4},{4,5},{5,6},{6,7},{8,9},{9,10},{10,11},{11... | collective-permute-start | bytes 294920 | tf_op jit(solution)/shard_map/ppermute | solution.py:17
  33.6 14.1 %collective-permute-start.7 = (bf16[96,4,1,128]{3,0,2,1:T(8,128)(2,1)S(1)}, bf16[96,4,1,128]{3,0,2,1:T(8,128)(2,1)S(1)}, u32[]{:S(2)}, u32[]{:S(2)}) collective-permute-start(bf16[96,4,1,128]{3,0,2,1:T(8,128)(2,1)S(1)} %get-tuple-element.54), channel_id=1, source_target_pairs={{1,0},{2,1},{3,2},{4,3},{5,4},{6,5},{7,6},{9,8},{10,9},{11,10},{12... | collective-permute-start | bytes 294920 | tf_op jit(solution)/shard_map/ppermute | solution.py:19
  35.0 8.6 %collective-permute-start.2 = (bf16[96,4,1,128]{3,0,2,1:T(8,128)(2,1)S(1)}, bf16[96,4,1,128]{3,0,2,1:T(8,128)(2,1)S(1)}, u32[]{:S(2)}, u32[]{:S(2)}) collective-permute-start(bf16[96,4,1,128]{3,0,2,1:T(8,128)(2,1)S(1)} %get-tuple-element.57), channel_id=1, source_target_pairs={{0,1},{1,2},{2,3},{3,4},{4,5},{5,6},{6,7},{8,9},{9,10},{10,11},{11... | collective-permute-start | bytes 294920 | tf_op jit(solution)/shard_map/ppermute | solution.py:17
  39.9 6.3 %collective-permute-start.3 = (bf16[96,4,1,128]{3,0,2,1:T(8,128)(2,1)S(1)}, bf16[96,4,1,128]{3,0,2,1:T(8,128)(2,1)S(1)}, u32[]{:S(2)}, u32[]{:S(2)}) collective-permute-start(bf16[96,4,1,128]{3,0,2,1:T(8,128)(2,1)S(1)} %get-tuple-element.58), channel_id=1, source_target_pairs={{1,0},{2,1},{3,2},{4,3},{5,4},{6,5},{7,6},{9,8},{10,9},{11,10},{12... | collective-permute-start | bytes 294920 | tf_op jit(solution)/shard_map/ppermute | solution.py:19
  90.4 9.3 %copy-start.26 = (bf16[96,2,8,128]{3,2,1,0:T(8,128)(2,1)S(1)}, bf16[96,2,8,128]{3,2,1,0:T(8,128)(2,1)}, u32[]{:S(2)}) copy-start(bf16[96,2,8,128]{3,2,1,0:T(8,128)(2,1)} %copy.54) | copy-start | bytes 1179652
  90.4 10.2 %copy-start.17 = (bf16[96,2,8,128]{3,2,1,0:T(8,128)(2,1)S(1)}, bf16[96,2,8,128]{3,2,1,0:T(8,128)(2,1)}, u32[]{:S(2)}) copy-start(bf16[96,2,8,128]{3,2,1,0:T(8,128)(2,1)} %copy.55) | copy-start | bytes 1179652
  90.4 11.0 %copy-start.25 = (bf16[96,2,8,128]{3,2,1,0:T(8,128)(2,1)S(1)}, bf16[96,2,8,128]{3,2,1,0:T(8,128)(2,1)}, u32[]{:S(2)}) copy-start(bf16[96,2,8,128]{3,2,1,0:T(8,128)(2,1)} %copy.56) | copy-start | bytes 1179652
  90.4 11.8 %copy-start.31 = (bf16[9,96,96]{2,1,0:T(8,128)(2,1)S(1)}, bf16[9,96,96]{2,1,0:T(8,128)(2,1)}, u32[]{:S(2)}) copy-start(bf16[9,96,96]{2,1,0:T(8,128)(2,1)} %get-tuple-element.63) | copy-start | bytes 497668
  100.5 4.8 %copy-start.3 = (bf16[864,2048]{1,0:T(8,128)(2,1)S(1)}, bf16[864,2048]{1,0:T(8,128)(2,1)}, u32[]{:S(2)}) copy-start(bf16[864,2048]{1,0:T(8,128)(2,1)} %bitcast_dynamic-update-slice_fusion.17) | copy-start | bytes 10616836
  100.6 4.8 %copy-start.16 = (bf16[96,2,8,128]{3,2,1,0:T(8,128)(2,1)S(1)}, bf16[96,2,8,128]{3,2,1,0:T(8,128)(2,1)}, u32[]{:S(2)}) copy-start(bf16[96,2,8,128]{3,2,1,0:T(8,128)(2,1)} %copy.58) | copy-start | bytes 1179652
  101.4 4.0 %copy-start.24 = (bf16[96,2,8,128]{3,2,1,0:T(8,128)(2,1)S(1)}, bf16[96,2,8,128]{3,2,1,0:T(8,128)(2,1)}, u32[]{:S(2)}) copy-start(bf16[96,2,8,128]{3,2,1,0:T(8,128)(2,1)} %copy.59) | copy-start | bytes 1179652
  102.2 3.5 %copy-start.22 = (bf16[96,2,8,128]{3,2,1,0:T(8,128)(2,1)S(1)}, bf16[96,2,8,128]{3,2,1,0:T(8,128)(2,1)}, u32[]{:S(2)}) copy-start(bf16[96,2,8,128]{3,2,1,0:T(8,128)(2,1)} %copy.62) | copy-start | bytes 1179652
  102.3 3.6 %copy-start.21 = (bf16[96,2,8,128]{3,2,1,0:T(8,128)(2,1)S(1)}, bf16[96,2,8,128]{3,2,1,0:T(8,128)(2,1)}, u32[]{:S(2)}) copy-start(bf16[96,2,8,128]{3,2,1,0:T(8,128)(2,1)} %copy.63) | copy-start | bytes 1179652
  106.4 3.4 %copy-start.1 = (bf16[864,2048]{1,0:T(8,128)(2,1)S(1)}, bf16[864,2048]{1,0:T(8,128)(2,1)}, u32[]{:S(2)}) copy-start(bf16[864,2048]{1,0:T(8,128)(2,1)} %copy-done) | copy-start | bytes 10616836
  106.4 3.5 %copy-start.6 = (f32[2048,96]{0,1:T(8,128)S(1)}, f32[2048,96]{0,1:T(8,128)}, u32[]{:S(2)}) copy-start(f32[2048,96]{0,1:T(8,128)} %fusion.23) | copy-start | bytes 2359300
  106.4 3.5 %copy-start.28 = (bf16[96,9,96]{0,2,1:T(8,128)(2,1)S(1)}, bf16[96,9,96]{0,2,1:T(8,128)(2,1)}, u32[]{:S(2)}) copy-start(bf16[96,9,96]{0,2,1:T(8,128)(2,1)} %copy.36) | copy-start | bytes 497668
  (18 other events, 36.9 us)
Sparse Core Ops, SparseCore 0:
  90.5 152.8 all-reduce.3
where the time goes:
time: 253 us
  waiting for transfers between devices  131 us (52%)
  local copies, waits for them, and re-layouts  58.9 us (23%)
  starting transfers between devices  25.1 us (10%)
  between operations  15 us (6%)
  matrix products  12.2 us (5%)
  other arithmetic  10.6 us (4%)
    psum x1, waiting for transfers between devices, shards(): weight_grad = lax.psum(weight_grad, ('gx', 'gy'))  128 us
    slice x28, local copies, waits for them, and re-layouts, shards(): padded_cot[:, 1 - plane_offset:1 - plane_offset + width_x, 2 - lane_y:2 -...  23.5 us
    unnamed x116, local copies, waits for them, and re-layouts  21.7 us
    ppermute x4, starting transfers between devices, with_halo(): lax.ppermute(tail, axis, [(i, (i + 1) % count) for i in range(ends)])  18.6 us
    ppermute x4, starting transfers between devices, with_halo(): lax.ppermute(head, axis, [((i + 1) % count, i) for i in range(ends)])  6.42 us
    slice x28, local copies, waits for them, and re-layouts, shards(): padded_in[:, 1 + plane_offset:1 + plane_offset + width_x, lane_y:lane_y +...  6.42 us
  transfers between devices with their start and end apart: 9, of which 2 were waited for; matrix products, arithmetic and copies ran while one was open for 12% of the time, Pallas kernels for 0%

commit v1 on v0

v1 whole, which is shorter than its diff:
```python
import math

import jax
import jax.numpy as jnp
from jax import lax
from jax.experimental import pallas as pl
from jax.experimental.pallas import tpu as pltpu
from jax.sharding import PartitionSpec as P

MESH = pl.DeviceIdType.MESH
F32 = jnp.float32
BF16 = jnp.bfloat16
C = 96
NX, NY, NZ = 2, 8, 128
TILES = 256
HALF = 128
NEAR, FAR, SAME = 0, 1, 2
NT = (((1,), (1,)), ((), ()))


def kernel(
    scale,
    feat, cot, w, ground, thick,
    out, grad_in, grad_w,
    pf, pc, tmp, shifted, lf, lb, acc, red, r0, r1, r2, r3, full, tout,
    halo_send, halo_recv, rs_send, rs_recv, ag_send, ag_recv, core_send, core_recv,
):
    gx = lax.axis_index("gx")
    gy = lax.axis_index("gy")
    core = lax.rem(gx, 2)
    y_hi = lax.rem(lax.div(gx, 2), 2)
    cx = lax.div(gx, 4)
    y_lo = lax.rem(gy, 2)
    cz = lax.div(gy, 2)
    cy = y_hi * 2 + y_lo
    near_gx = gx + 1 - 2 * core
    far_gx = gx - 1 + 2 * core
    has_far = jnp.logical_and(far_gx >= 0, far_gx < 16)
    x_first = 1 - core

    def chip(x, y, z):
        return (x * 4 + lax.div(y, 2) * 2 + core, z * 2 + lax.rem(y, 2))

    def peer(stage, d):
        first = 1 - core if stage == 1 else core
        if stage == 3:
            return chip(cx, lax.rem(cy + d, 4), cz)
        return chip(lax.rem(cx + d * first, 4), cy, lax.rem(cz + d * (1 - first), 4))

    pos = {
        1: cx * (1 - core) + cz * core,
        2: cz * (1 - core) + cx * core,
        3: cy,
    }

    has_dy = {-1: gy > 0, 0: None, 1: gy < 7}

    def present(side, dy):
        terms = []
        if side == FAR:
            terms.append(has_far)
        if dy != 0:
            terms.append(has_dy[dy])
        if not terms:
            return None
        return terms[0] if len(terms) == 1 else jnp.logical_and(*terms)

    def when(cond, fn):
        if cond is None:
            fn()
        else:
            pl.when(cond)(fn)

    def halo_device(side, dy):
        return ({NEAR: near_gx, FAR: far_gx, SAME: gx}[side], gy + dy)

    halos = [(s, dy) for s in (FAR, NEAR, SAME) for dy in (0, -1, 1) if (s, dy) != (SAME, 0)]

    barrier = pltpu.get_barrier_semaphore()
    for side, dy in halos:
        def greet(side=side, dy=dy):
            pl.semaphore_signal(barrier, inc=1, device_id=halo_device(side, dy), device_id_type=MESH)
        when(present(side, dy), greet)
    pl.semaphore_signal(barrier, inc=1, device_id=(near_gx, gy), device_id_type=MESH)
    for stage in (1, 2, 3):
        for d in (1, 2, 3):
            pl.semaphore_signal(barrier, inc=1, device_id=peer(stage, d), device_id_type=MESH)

    rows = lax.broadcasted_iota(jnp.int32, (NY, NZ), 0)
    heights = lax.broadcasted_iota(jnp.int32, (NY, NZ), 1)

    def occupied(x):
        low = jnp.zeros((NY, NZ), jnp.int32)
        high = jnp.zeros((NY, NZ), jnp.int32)
        for y in range(NY):
            g = ground[x, y]
            low = jnp.where(rows == y, g, low)
            high = jnp.where(rows == y, g + thick[x, y], high)
        return jnp.logical_and(heights >= low, heights < high)

    occ = [occupied(x) for x in range(NX)]

    def columns(src, dst, x, shifts):
        value = jnp.where(occ[x][None], src[:, x].astype(F32), 0.0)
        tmp[...] = value.reshape(C * NY, NZ)
        for y in range(NY):
            col = tmp[pl.ds(y, C, stride=NY), :]
            dst[x + 1, y + 1] = col.astype(BF16)
            if shifts:
                lanes = slice(y * NZ, (y + 1) * NZ)
                shifted[x, 0:C, lanes] = pltpu.roll(col, NZ - 1, 1).astype(BF16)
                shifted[x, C : 2 * C, lanes] = col.astype(BF16)
                shifted[x, 2 * C : 3 * C, lanes] = pltpu.roll(col, 1, 1).astype(BF16)

    for x in range(NX):
        columns(feat, pf, x, False)

    n_dy = jnp.where(gy > 0, 1, 0) + jnp.where(gy < 7, 1, 0)
    n_far = jnp.where(has_far, 1, 0)
    pl.semaphore_wait(barrier, (n_dy + 1) * (2 + n_far) - 1 + 10)

    src_y = {-1: 1, 0: 1, 1: NY}
    dst_y = {-1: NY + 1, 0: 1, 1: 0}
    len_y = {-1: 1, 0: NY, 1: 1}

    def halo_copy(which, side, dy):
        buf = (pf, pc)[which]
        n = len_y[dy]
        if side == SAME:
            src_x = dst_x = pl.ds(1, 2)
        elif side == NEAR:
            src_x, dst_x = pl.ds(2 - core, 1), pl.ds(3 * core, 1)
        else:
            src_x, dst_x = pl.ds(1 + core, 1), pl.ds(3 * (1 - core), 1)
        return pltpu.make_async_remote_copy(
            src_ref=buf.at[src_x, pl.ds(src_y[dy], n)],
            dst_ref=buf.at[dst_x, pl.ds(dst_y[dy], n)],
            send_sem=halo_send.at[which, side, dy + 1],
            recv_sem=halo_recv.at[which, side, dy + 1],
            device_id=halo_device(side, dy),
            device_id_type=MESH,
        )

    def send_halos(which):
        for side, dy in halos:
            when(present(side, dy), lambda side=side, dy=dy: halo_copy(which, side, dy).start())

    def recv_halos(which, sides):
        for side, dy in halos:
            if side in sides:
                when(present(side, -dy), lambda side=side, dy=dy: halo_copy(which, side, dy).wait_recv())

    def done_halos(which):
        for side, dy in halos:
            when(present(side, dy), lambda side=side, dy=dy: halo_copy(which, side, dy).wait_send())

    def clear_edges(buf):
        zeros = jnp.zeros((C, NZ), BF16)

        def far_side():
            for y in range(NY + 2):
                buf[3 * core, y] = zeros

        def y_side(y):
            for x in range(NX + 2):
                buf[x, y] = zeros

        pl.when(jnp.logical_not(has_far))(far_side)
        pl.when(gy == 0)(lambda: y_side(0))
        pl.when(gy == 7)(lambda: y_side(NY + 1))

    send_halos(0)
    for x in range(NX):
        columns(cot, pc, x, True)
    clear_edges(pf)
    clear_edges(pc)

    for c in range(3):
        lf[c * C : (c + 1) * C, :] = jnp.concatenate([w[ab * 3 + c] for ab in range(9)], axis=1)
        lb[c * C : (c + 1) * C, :] = jnp.concatenate(
            [w[26 - (ab * 3 + c)].T for ab in range(9)], axis=1
        )

    def weight_terms(x):
        stack = jnp.concatenate(
            [
                jnp.concatenate([pf[x + a, y + b] for y in range(NY)], axis=1)
                for a in range(3)
                for b in range(3)
            ],
            axis=0,
        )
        return lax.dot_general(shifted[x], stack, NT, preferred_element_type=F32)

    recv_halos(0, (NEAR, SAME))
    acc[...] = weight_terms(x_first)
    recv_halos(0, (FAR,))
    send_halos(1)
    total = acc[...] + weight_terms(1 - x_first)
    for i in range(36):
        for j in range(7):
            tile = total[i * 8 : (i + 1) * 8, j * 128 : min((j + 1) * 128, 9 * C)]
            if j == 6:
                tile = jnp.concatenate([tile, jnp.zeros((8, 32), F32)], axis=1)
            red[i * 7 + j] = tile
    red[252:256] = jnp.zeros((4, 8, 128), F32)

    def conv_pair(x, j, buf, lhs):
        stack = jnp.concatenate(
            [
                jnp.concatenate([buf[x + a, 2 * j + b], buf[x + a, 2 * j + b + 1]], axis=1)
                for a in range(3)
                for b in range(3)
            ],
            axis=0,
        )
        prod = jnp.dot(lhs[...], stack, preferred_element_type=F32)
        for half in range(2):
            part = prod[:, half * NZ : (half + 1) * NZ]
            col = (
                pltpu.roll(part[0:C], 1, 1) + part[C : 2 * C] + pltpu.roll(part[2 * C : 3 * C], NZ - 1, 1)
            )
            tout[pl.ds(2 * j + half, C, stride=NY), :] = col

    def conv(x, buf, lhs, dst):
        for j in range(NY // 2):
            conv_pair(x, j, buf, lhs)
        mask = occupied(x)
        dst[:, x] = jnp.where(mask[None], tout[...].reshape(C, NY, NZ), 0.0).astype(BF16)

    core_device = (near_gx, gy)

    def core_copy(k, src, dst):
        return pltpu.make_async_remote_copy(
            src_ref=src, dst_ref=dst, send_sem=core_send.at[k], recv_sem=core_recv.at[k],
            device_id=core_device, device_id_type=MESH,
        )

    mine = core * HALF
    first = core_copy(0, red.at[pl.ds((1 - core) * HALF, HALF)], r0)
    first.start()
    recv_halos(1, (NEAR, SAME))
    conv(x_first, pf, lf, out)
    first.wait_recv()
    red[pl.ds(mine, HALF)] = red[pl.ds(mine, HALF)] + r0[...]

    size = HALF
    base = mine
    boxes = {1: r1, 2: r2, 3: r3}
    bases = {}
    sent = [first]
    work = {
        1: lambda: conv(1 - x_first, pf, lf, out),
        2: lambda: conv(x_first, pc, lb, grad_in),
        3: lambda: (recv_halos(1, (FAR,)), conv(1 - x_first, pc, lb, grad_in)),
    }
    for stage in (1, 2, 3):
        size //= 4
        copies = []
        for d in (1, 2, 3):
            target = lax.rem(pos[stage] + d, 4)
            copies.append(
                pltpu.make_async_remote_copy(
                    src_ref=red.at[pl.ds(base + target * size, size)],
                    dst_ref=boxes[stage].at[d - 1],
                    send_sem=rs_send.at[stage - 1, d - 1],
                    recv_sem=rs_recv.at[stage - 1, d - 1],
                    device_id=peer(stage, d),
                    device_id_type=MESH,
                )
            )
        for copy in copies:
            copy.start()
        sent += copies
        work[stage]()
        base = base + pos[stage] * size
        bases[stage] = base
        total = red[pl.ds(base, size)]
        for d in (1, 2, 3):
            copies[d - 1].wait_recv()
            total = total + boxes[stage][d - 1]
        if stage < 3:
            red[pl.ds(base, size)] = total
        else:
            full[pl.ds(base, size)] = total * scale

    for stage in (3, 2, 1):
        here = full.at[pl.ds(bases[stage], size)]
        copies = [
            pltpu.make_async_remote_copy(
                src_ref=here, dst_ref=here,
                send_sem=ag_send.at[stage - 1, d - 1],
                recv_sem=ag_recv.at[stage - 1, d - 1],
                device_id=peer(stage, d),
                device_id_type=MESH,
            )
            for d in (1, 2, 3)
        ]
        for copy in copies:
            copy.start()
        for copy in copies:
            copy.wait_recv()
        sent += copies
        size *= 4
    mine_full = full.at[pl.ds(mine, HALF)]
    last = core_copy(1, mine_full, mine_full)
    last.start()
    sent.append(last)
    done_halos(0)
    done_halos(1)
    last.wait_recv()

    for i in range(36):
        row = jnp.concatenate([full[i * 7 + j] for j in range(7)], axis=1)
        c, o = i // 12, (i % 12) * 8
        for ab in range(9):
            grad_w[ab * 3 + c, o : o + 8, :] = row[:, ab * C : (ab + 1) * C]
    for copy in sent:
        copy.wait_send()


def shards(features, cotangent, weights, ground, thick):
    voxels = NX * NY * NZ * lax.axis_size("gx") * lax.axis_size("gy")
    block = jax.ShapeDtypeStruct((C, NX, NY, NZ), BF16)
    vmem = pl.BlockSpec(memory_space=pltpu.VMEM)
    smem = pl.BlockSpec(memory_space=pltpu.SMEM)

    def body(*refs):
        kernel(1.0 / math.sqrt(voxels), *refs)

    return pl.pallas_call(
        body,
        out_shape=(block, block, jax.ShapeDtypeStruct((27, C, C), F32)),
        in_specs=[vmem, vmem, vmem, smem, smem],
        out_specs=(vmem, vmem, vmem),
        scratch_shapes=[
            pltpu.VMEM((NX + 2, NY + 2, C, NZ), BF16),
            pltpu.VMEM((NX + 2, NY + 2, C, NZ), BF16),
            pltpu.VMEM((C * NY, NZ), F32),
            pltpu.VMEM((NX, 3 * C, NY * NZ), BF16),
            pltpu.VMEM((3 * C, 9 * C), BF16),
            pltpu.VMEM((3 * C, 9 * C), BF16),
            pltpu.VMEM((3 * C, 9 * C), F32),
            pltpu.VMEM((TILES, 8, 128), F32),
            pltpu.VMEM((HALF, 8, 128), F32),
            pltpu.VMEM((3, HALF // 4, 8, 128), F32),
            pltpu.VMEM((3, HALF // 16, 8, 128), F32),
            pltpu.VMEM((3, HALF // 64, 8, 128), F32),
            pltpu.VMEM((TILES, 8, 128), F32),
            pltpu.VMEM((C * NY, NZ), F32),
            pltpu.SemaphoreType.DMA((2, 3, 3)),
            pltpu.SemaphoreType.DMA((2, 3, 3)),
            pltpu.SemaphoreType.DMA((3, 3)),
            pltpu.SemaphoreType.DMA((3, 3)),
            pltpu.SemaphoreType.DMA((3, 3)),
            pltpu.SemaphoreType.DMA((3, 3)),
            pltpu.SemaphoreType.DMA((2,)),
            pltpu.SemaphoreType.DMA((2,)),
        ],
        compiler_params=pltpu.CompilerParams(
            collective_id=0, has_side_effects=True, vmem_limit_bytes=56 * 1024 * 1024
        ),
        cost_estimate=pl.CostEstimate(
            flops=3 * 2 * NX * NY * NZ * 27 * C * C, bytes_accessed=4 * 2**20, transcendentals=0
        ),
    )(features, cotangent, weights, ground, thick)


def solution(mesh):
    assert mesh.shape["gx"] == 16 and mesh.shape["gy"] == 8
    placed = (
        P(None, "gx", "gy", None),
        P(None, "gx", "gy", None),
        P(),
        P("gx", "gy"),
        P("gx", "gy"),
    )
    return jax.shard_map(
        shards,
        mesh=mesh,
        in_specs=placed,
        out_specs=(P(None, "gx", "gy", None), P(None, "gx", "gy", None), P()),
        check_vma=False,
    )
```

time: 253 us -> 65.7 us (0.26)
  waiting for transfers between devices: 131 us -> 0 us
  Pallas kernels: 0 us -> 60.1 us
  local copies, waits for them, and re-layouts: 58.9 us -> 4.7 us
  starting transfers between devices: 25.1 us -> 0 us
  between operations: 15 us -> 0.65 us
  matrix products: 12.2 us -> 0 us
  other arithmetic: 10.6 us -> 0 us
    psum x1 -> x0, waiting for transfers between devices: 128 us -> none  [shards(): weight_grad = lax.psum(weight_grad, ('gx', 'gy'))]
    pallas_call x0 -> x1, Pallas kernels: none -> 60.1 us  [shards(): pl.pallas_call(body, out_shape=(block, block, jax.ShapeDtypeStruct((27, C...]
    slice x59 -> x0, local copies, waits for them, and re-layouts: 32.5 us -> none  [the longest x28 23.5 us: shards(): padded_cot[:, 1 - plane_offset:1 - plane_offset + width_x, 2 - lane_y:2 -...]
    ppermute x8 -> x0, starting transfers between devices: 25 us -> none  [the longest x4 18.6 us: with_halo(): lax.ppermute(tail, axis, [(i, (i + 1) % count) for i in range(ends)])]
    unnamed x116 -> x5, local copies, waits for them, and re-layouts: 21.7 us -> 4.7 us
    dot_general x9 -> x0, matrix products: 12.2 us -> none  [the longest x3 4.58 us: shards(): jnp.dot(backward_matrix, backward_stack, preferred_element_type=jnp.float32)]
    concatenate x7 -> x0, other arithmetic: 5.24 us -> none  [the longest x6 4.07 us: with_halo(): jnp.concatenate([lax.ppermute(tail, axis, [(i, (i + 1) % count) for i in...]
    mul x2 -> x0, other arithmetic: 3.77 us -> none  [the longest x1 2.48 us: shards(): weight_grad = weight_grad * grad_scale]
  transfers between devices with their start and end apart: 9 -> 0, of which waited for: 2 -> 0; matrix products, arithmetic and copies ran while one was open for 12% -> 0% of each run, Pallas kernels for 0% -> 0%
where the time goes in v1:
time: 65.7 us; the launch traced here: 65.5 us
  Pallas kernels  60.1 us (91%)
  local copies, waits for them, and re-layouts  4.7 us (7%)
    pallas_call x1, Pallas kernels, shards(): pl.pallas_call(body, out_shape=(block, block, jax.ShapeDtypeStruct((27, C...  60.1 us
    unnamed x5, local copies, waits for them, and re-layouts  4.7 us

profile of v1, /device:TPU:1, one launch (start us, length us, event | category | flops | bytes accessed | tf_op | source)
XLA Modules:
  0.0 65.5 jit_solution(11887380170441368427)
XLA Ops:
  0.6 60.1 %shard_map.76 = (bf16[96,2,8,128]{3,2,1,0:T(8,128)(2,1)}, bf16[96,2,8,128]{3,2,1,0:T(8,128)(2,1)}, f32[27,96,96]{2,1,0:T(8,128)}) custom-call(bf16[96,2,8,128]{3,2,1,0:T(8,128)(2,1)} %refs_0_.1, bf16[96,2,8,128]{3,2,1,0:T(8,128)(2,1)} %refs_1_.1, bf16[27,96,96]{2,1,0:T(8,128)(2,1)} %refs_2_.1, s32[2,8]{1,0:T(2,128)} %refs_3_.1, s32[2,8]{1,0:T(2,128)} %refs_4_.1), custom_call_target="tpu_custom_call" | custom-call | flops 3057647616 | bytes 4194304 | tf_op jit(solution)/shard_map/pallas_call | solution.py:331
  60.8 0.0 copy-start
  60.8 1.9 %copy.11 = bf16[96,2,8,128]{3,2,1,0:T(8,128)(2,1)} copy(bf16[96,2,8,128]{3,2,1,0:T(8,128)(2,1)} %get-tuple-element.6) | data formatting | bytes 786432
  62.7 1.8 %copy.12 = bf16[96,2,8,128]{3,2,1,0:T(8,128)(2,1)} copy(bf16[96,2,8,128]{3,2,1,0:T(8,128)(2,1)} %get-tuple-element.7) | data formatting | bytes 786432
  64.4 0.0 copy-done
  64.4 1.1 %copy.13 = f32[27,96,96]{2,1,0:T(8,128)} copy(f32[27,96,96]{2,1,0:T(8,128)S(1)} %copy-done) | data formatting | bytes 1990656
Async XLA Ops:
  60.8 3.6 %copy-start = (f32[27,96,96]{2,1,0:T(8,128)S(1)}, f32[27,96,96]{2,1,0:T(8,128)}, u32[]{:S(2)}) copy-start(f32[27,96,96]{2,1,0:T(8,128)} %get-tuple-element.8) | copy-start | bytes 2985988

commit v2 on v1

v2 whole, which is shorter than its diff:
```python
import math

import jax
import jax.numpy as jnp
from jax import lax
from jax.experimental import pallas as pl
from jax.experimental.pallas import tpu as pltpu
from jax.sharding import PartitionSpec as P

MESH = pl.DeviceIdType.MESH
F32 = jnp.float32
BF16 = jnp.bfloat16
C = 96
NX, NY, NZ = 2, 8, 128
OWNERS = 54
LANES = 128
NEAR, FAR, SAME = 0, 1, 2
NT = (((1,), (1,)), ((), ()))


def kernel(
    scale,
    feat_hbm, cot_hbm, w_hbm, ground, thick,
    out_hbm, grad_in_hbm, grad_w_hbm,
    feat, cot, w, out, grad_in, pf, pc, tmp, shifted, lf, lb, red, core_box, late_box, mid_box, full, tout,
    load_sem, store_sem, halo_send, halo_recv, core_send, core_recv,
    rs_send, rs_recv, ag_send, ag_recv, plane_sem, cube_sem,
):
    gx = lax.axis_index("gx")
    gy = lax.axis_index("gy")
    core = lax.rem(gx, 2)
    cx = lax.div(gx, 4)
    cy = lax.rem(lax.div(gx, 2), 2) * 2 + lax.rem(gy, 2)
    cz = lax.div(gy, 2)
    near_gx = gx + 1 - 2 * core
    far_gx = gx - 1 + 2 * core
    has_far = jnp.logical_and(far_gx >= 0, far_gx < 16)
    near_x = 1 - core
    far_x = core
    near_a = 2 * (1 - core)
    far_a = 2 * core

    loads = [
        pltpu.make_async_copy(feat_hbm, feat, load_sem.at[0]),
        pltpu.make_async_copy(cot_hbm, cot, load_sem.at[1]),
        pltpu.make_async_copy(w_hbm, w, load_sem.at[2]),
    ]
    for load in loads:
        load.start()

    def chip(x, y, z):
        return (x * 4 + lax.div(y, 2) * 2 + core, z * 2 + lax.rem(y, 2))

    def step(dx, dy, dz):
        return lax.rem(cx + dx, 4), lax.rem(cy + dy, 4), lax.rem(cz + dz, 4)

    has_dy = {-1: gy > 0, 0: None, 1: gy < 7}

    def present(side, dy):
        terms = []
        if side == FAR:
            terms.append(has_far)
        if dy != 0:
            terms.append(has_dy[dy])
        if not terms:
            return None
        return terms[0] if len(terms) == 1 else jnp.logical_and(*terms)

    def when(cond, fn):
        if cond is None:
            fn()
        else:
            pl.when(cond)(fn)

    def halo_device(side, dy):
        return ({NEAR: near_gx, FAR: far_gx, SAME: gx}[side], gy + dy)

    halos = [(s, dy) for s in (FAR, SAME, NEAR) for dy in (0, -1, 1) if (s, dy) != (SAME, 0)]
    rings = {
        "x": [chip(*step(d, 0, 0)) for d in (1, 2, 3)],
        "y": [chip(*step(0, d, 0)) for d in (1, 2, 3)],
        "z": [chip(*step(0, 0, d)) for d in (1, 2, 3)],
    }

    def signal(sem, device):
        pl.semaphore_signal(sem, inc=1, device_id=device, device_id_type=MESH)

    barrier = pltpu.get_barrier_semaphore()
    for side, dy in halos:
        when(present(side, dy), lambda side=side, dy=dy: signal(barrier, halo_device(side, dy)))
    for axis in "xyz":
        for device in rings[axis]:
            signal(barrier, device)

    rows = lax.broadcasted_iota(jnp.int32, (NY, NZ), 0)
    heights = lax.broadcasted_iota(jnp.int32, (NY, NZ), 1)

    def occupied(x):
        low = jnp.zeros((NY, NZ), jnp.int32)
        high = jnp.zeros((NY, NZ), jnp.int32)
        for y in range(NY):
            g = ground[x, y]
            low = jnp.where(rows == y, g, low)
            high = jnp.where(rows == y, g + thick[x, y], high)
        return jnp.logical_and(heights >= low, heights < high)

    def columns(src, dst, x, shifts):
        value = jnp.where(occupied(x)[None], src[:, x].astype(F32), 0.0)
        tmp[...] = value.reshape(C * NY, NZ)
        for y in range(NY):
            col = tmp[pl.ds(y, C, stride=NY), :]
            dst[x + 1, y + 1] = col.astype(BF16)
            if shifts:
                lanes = slice(y * NZ, (y + 1) * NZ)
                shifted[x, 0:C, lanes] = pltpu.roll(col, NZ - 1, 1).astype(BF16)
                shifted[x, C : 2 * C, lanes] = col.astype(BF16)
                shifted[x, 2 * C : 3 * C, lanes] = pltpu.roll(col, 1, 1).astype(BF16)

    loads[0].wait()
    for x in range(NX):
        columns(feat, pf, x, False)

    n_dy = jnp.where(gy > 0, 1, 0) + jnp.where(gy < 7, 1, 0)
    n_far = jnp.where(has_far, 1, 0)
    pl.semaphore_wait(barrier, (n_dy + 1) * (2 + n_far) - 1 + 9)

    src_y = {-1: 1, 0: 1, 1: NY}
    dst_y = {-1: NY + 1, 0: 1, 1: 0}
    len_y = {-1: 1, 0: NY, 1: 1}

    def halo_copy(which, side, dy):
        buf = (pf, pc)[which]
        n = len_y[dy]
        if side == SAME:
            src_x = dst_x = pl.ds(1, 2)
        elif side == NEAR:
            src_x, dst_x = pl.ds(2 - core, 1), pl.ds(3 * core, 1)
        else:
            src_x, dst_x = pl.ds(1 + core, 1), pl.ds(3 * (1 - core), 1)
        return pltpu.make_async_remote_copy(
            src_ref=buf.at[src_x, pl.ds(src_y[dy], n)],
            dst_ref=buf.at[dst_x, pl.ds(dst_y[dy], n)],
            send_sem=halo_send.at[which, side, dy + 1],
            recv_sem=halo_recv.at[which, side, dy + 1],
            device_id=halo_device(side, dy),
            device_id_type=MESH,
        )

    def send_halos(which):
        for side, dy in halos:
            when(present(side, dy), lambda side=side, dy=dy: halo_copy(which, side, dy).start())

    def recv_halos(which, sides):
        for side, dy in halos:
            if side in sides:
                when(present(side, -dy), lambda side=side, dy=dy: halo_copy(which, side, dy).wait_recv())

    def done_halos(which, sides):
        for side, dy in halos:
            if side in sides:
                when(present(side, dy), lambda side=side, dy=dy: halo_copy(which, side, dy).wait_send())

    def clear_edges(buf):
        zeros = jnp.zeros((C, NZ), BF16)

        def far_side():
            for y in range(NY + 2):
                buf[3 * core, y] = zeros

        def y_side(y):
            for x in range(NX + 2):
                buf[x, y] = zeros

        pl.when(jnp.logical_not(has_far))(far_side)
        pl.when(gy == 0)(lambda: y_side(0))
        pl.when(gy == 7)(lambda: y_side(NY + 1))

    send_halos(0)
    for device in rings["z"]:
        signal(plane_sem, device)
    loads[1].wait()
    for x in range(NX):
        columns(cot, pc, x, True)
    send_halos(1)
    clear_edges(pf)
    clear_edges(pc)
    pl.semaphore_wait(plane_sem, 3)
    for device in rings["y"]:
        signal(cube_sem, device)

    loads[2].wait()
    for c in range(3):
        lf[c * C : (c + 1) * C, :] = jnp.concatenate([w[ab * 3 + c] for ab in range(9)], axis=1)
        lb[c * C : (c + 1) * C, :] = jnp.concatenate(
            [w[26 - (ab * 3 + c)].T for ab in range(9)], axis=1
        )

    def weight_terms(xs, a, b):
        lhs = jnp.concatenate([shifted[x] for x in xs], axis=1)
        rhs = jnp.concatenate([pf[x + a, y + b] for x in xs for y in range(NY)], axis=1)
        return lax.dot_general(lhs, rhs, NT, preferred_element_type=F32)

    def put(a, b, value, add):
        for c in range(3):
            k = a * 9 + b * 3 + c
            part = value[c * C : (c + 1) * C]
            red[k, :, 0:C] = red[k, :, 0:C] + part if add else part

    recv_halos(0, (NEAR, SAME))
    for b in range(3):
        put(near_a, b, weight_terms((near_x, far_x), near_a, b), False)
    for b in range(3):
        put(1, b, weight_terms((near_x, far_x), 1, b), False)

    def core_copy(k, src, dst):
        return pltpu.make_async_remote_copy(
            src_ref=src, dst_ref=dst, send_sem=core_send.at[k], recv_sem=core_recv.at[k],
            device_id=(near_gx, gy), device_id_type=MESH,
        )

    other = 1 - core

    def core_parts(m):
        return [
            (pl.ds(18 * m, 9), slice(None), pl.ds(0, 9)),
            (pl.ds(9 + 5 * m, 4), slice(None), pl.ds(9, 4)),
            (pl.ds(13, 1), pl.ds(48 * m, 48), pl.ds(13, 1)),
        ]

    pairs = []
    for i, (ks, rs, box) in enumerate(core_parts(other)):
        dst = core_box.at[box] if i < 2 else core_box.at[box, pl.ds(0, 48)]
        src = red.at[ks] if i < 2 else red.at[ks, rs]
        pairs.append(core_copy(i, src, dst))
    for pair in pairs:
        pair.start()
    for b in range(3):
        put(far_a, b, weight_terms((near_x,), far_a, b), False)

    def conv_pair(x, j, buf, lhs):
        stack = jnp.concatenate(
            [
                jnp.concatenate([buf[x + a, 2 * j + b], buf[x + a, 2 * j + b + 1]], axis=1)
                for a in range(3)
                for b in range(3)
            ],
            axis=0,
        )
        prod = jnp.dot(lhs[...], stack, preferred_element_type=F32)
        for half in range(2):
            part = prod[:, half * NZ : (half + 1) * NZ]
            col = (
                pltpu.roll(part[0:C], 1, 1) + part[C : 2 * C] + pltpu.roll(part[2 * C : 3 * C], NZ - 1, 1)
            )
            tout[pl.ds(2 * j + half, C, stride=NY), :] = col

    def conv(x, buf, lhs, dst):
        for j in range(NY // 2):
            conv_pair(x, j, buf, lhs)
        mask = occupied(x)
        dst[:, x] = jnp.where(mask[None], tout[...].reshape(C, NY, NZ), 0.0).astype(BF16)

    me = cx * 16 + cy * 4 + cz

    def late_share(buf, j):
        return buf.at[far_a * 9 + lax.div(j, 6), pl.ds(pl.multiple_of(lax.rem(j, 6) * 16, 16), 16)]

    def mid_share(buf, j):
        t = 54 * core + j
        return buf.at[9 + lax.div(t, 12), pl.ds(pl.multiple_of(lax.rem(t, 12) * 8, 8), 8)]

    others = sorted(
        [(dx, dy, dz) for dx in range(4) for dy in range(4) for dz in range(4) if (dx, dy, dz) != (0, 0, 0)],
        key=lambda d: -sum(min(v, 4 - v) for v in d),
    )

    def exchange(index, share, box):
        for dx, dy, dz in others:
            x, y, z = step(dx, dy, dz)
            j = x * 16 + y * 4 + z

            @pl.when(j < OWNERS)
            def _(x=x, y=y, z=z, j=j, d=dx * 16 + dy * 4 + dz):
                pltpu.make_async_remote_copy(
                    src_ref=share(red, j), dst_ref=box.at[d],
                    send_sem=rs_send.at[index], recv_sem=rs_recv.at[index],
                    device_id=chip(x, y, z), device_id_type=MESH,
                ).start()

    def drain(ref, sem):
        pltpu.make_async_copy(ref, ref, sem).wait()

    def collect(index, share, box):
        @pl.when(me < OWNERS)
        def _():
            drain(box.at[pl.ds(1, 63)], rs_recv.at[index])
            total = share(red, me)[...] + jnp.sum(box[1:64], axis=0)
            share(full, me)[...] = total * scale
            for dx, dy, dz in others:
                x, y, z = step(dx, dy, dz)
                pltpu.make_async_remote_copy(
                    src_ref=share(full, me), dst_ref=share(full, me),
                    send_sem=ag_send.at[index], recv_sem=ag_recv.at[index],
                    device_id=chip(x, y, z), device_id_type=MESH,
                ).start()

    def shares_wait(sem, box, n):
        drain(box.at[pl.ds(0, n)], sem)

    def gathered(sem, box):
        pl.when(me < OWNERS)(lambda: shares_wait(sem, box, OWNERS - 1))
        pl.when(me >= OWNERS)(lambda: shares_wait(sem, box, OWNERS))

    conv(near_x, pf, lf, out)
    for pair in pairs:
        pair.wait_recv()
    for i, (ks, rs, box) in enumerate(core_parts(core)):
        if i < 2:
            red[ks] = red[ks] + core_box[box]
        else:
            red[ks, rs] = red[ks, rs] + core_box[box, 0:48]
    pl.semaphore_wait(cube_sem, 3)
    exchange(0, mid_share, mid_box)
    recv_halos(0, (FAR,))
    for b in range(3):
        put(far_a, b, weight_terms((far_x,), far_a, b), True)
    exchange(1, late_share, late_box)
    conv(far_x, pf, lf, out)
    stores = [pltpu.make_async_copy(out, out_hbm, store_sem.at[0])]
    stores[0].start()
    recv_halos(1, (NEAR, SAME))
    conv(near_x, pc, lb, grad_in)
    collect(0, mid_share, mid_box)
    collect(1, late_share, late_box)
    recv_halos(1, (FAR,))
    conv(far_x, pc, lb, grad_in)
    stores.append(pltpu.make_async_copy(grad_in, grad_in_hbm, store_sem.at[1]))
    stores[1].start()

    gathered(ag_recv.at[0], mid_box)
    gathered(ag_recv.at[1], late_box)
    finals = []
    for i, (ks, rs, _) in enumerate(core_parts(core)):
        ref = full.at[ks] if i < 2 else full.at[ks, rs]
        finals.append(core_copy(3 + i, ref, ref))
    for copy in finals:
        copy.start()
    done_halos(0, (NEAR, SAME, FAR))
    done_halos(1, (NEAR, SAME, FAR))
    for copy in pairs:
        copy.wait_send()
    for index, box in enumerate((mid_box, late_box)):
        gathered(rs_send.at[index], box)
        pl.when(me < OWNERS)(lambda index=index, box=box: shares_wait(ag_send.at[index], box, 63))
    for copy in finals:
        copy.wait_recv()
    stores.append(pltpu.make_async_copy(full, grad_w_hbm, store_sem.at[2]))
    stores[2].start()
    for copy in finals:
        copy.wait_send()
    for store in stores:
        store.wait()


def hand_on(a, b, c, x, y, z, va, vb, vc, vz, load_sem, store_sem):
    loads = [
        pltpu.make_async_copy(src, dst, load_sem.at[i]) for i, (src, dst) in enumerate(((c, vc), (a, va), (b, vb)))
    ]
    stores = [
        pltpu.make_async_copy(src, dst, store_sem.at[i]) for i, (src, dst) in enumerate(((vz, z), (va, x), (vb, y)))
    ]
    for load in loads:
        load.start()
    loads[0].wait()
    vz[...] = vc[:, :, 0:C]
    for i in range(3):
        if i:
            loads[i].wait()
        stores[i].start()
    for store in stores:
        store.wait()


def shards(features, cotangent, weights, ground, thick):
    voxels = NX * NY * NZ * lax.axis_size("gx") * lax.axis_size("gy")
    block = jax.ShapeDtypeStruct((C, NX, NY, NZ), BF16)
    shapes = (block, block, jax.ShapeDtypeStruct((27, C, C), F32))
    hbm = pl.BlockSpec(memory_space=pl.ANY)
    smem = pl.BlockSpec(memory_space=pltpu.SMEM)

    def body(*refs):
        kernel(1.0 / math.sqrt(voxels), *refs)

    dma = pltpu.SemaphoreType.DMA
    results = pl.pallas_call(
        body,
        out_shape=(block, block, jax.ShapeDtypeStruct((27, C, LANES), F32)),
        in_specs=[hbm, hbm, hbm, smem, smem],
        out_specs=(hbm, hbm, hbm),
        scratch_shapes=[
            pltpu.VMEM((C, NX, NY, NZ), BF16),
            pltpu.VMEM((C, NX, NY, NZ), BF16),
            pltpu.VMEM((27, C, C), BF16),
            pltpu.VMEM((C, NX, NY, NZ), BF16),
            pltpu.VMEM((C, NX, NY, NZ), BF16),
            pltpu.VMEM((NX + 2, NY + 2, C, NZ), BF16),
            pltpu.VMEM((NX + 2, NY + 2, C, NZ), BF16),
            pltpu.VMEM((C * NY, NZ), F32),
            pltpu.VMEM((NX, 3 * C, NY * NZ), BF16),
            pltpu.VMEM((3 * C, 9 * C), BF16),
            pltpu.VMEM((3 * C, 9 * C), BF16),
            pltpu.VMEM((27, C, LANES), F32),
            pltpu.VMEM((14, C, LANES), F32),
            pltpu.VMEM((64, 16, LANES), F32),
            pltpu.VMEM((64, 8, LANES), F32),
            pltpu.VMEM((27, C, LANES), F32),
            pltpu.VMEM((C * NY, NZ), F32),
            dma((3,)),
            dma((3,)),
            dma((2, 3, 3)),
            dma((2, 3, 3)),
            dma((6,)),
            dma((6,)),
            dma((2,)),
            dma((2,)),
            dma((2,)),
            dma((2,)),
            pltpu.SemaphoreType.REGULAR,
            pltpu.SemaphoreType.REGULAR,
        ],
        compiler_params=pltpu.CompilerParams(
            collective_id=0, has_side_effects=True, vmem_limit_bytes=56 * 1024 * 1024
        ),
        cost_estimate=pl.CostEstimate(
            flops=3 * 2 * NX * NY * NZ * 27 * C * C, bytes_accessed=4 * 2**20, transcendentals=0
        ),
    )(features, cotangent, weights, ground, thick)
    return pl.pallas_call(
        hand_on,
        out_shape=shapes,
        in_specs=[hbm] * 3,
        out_specs=(hbm,) * 3,
        scratch_shapes=[
            pltpu.VMEM((C, NX, NY, NZ), BF16),
            pltpu.VMEM((C, NX, NY, NZ), BF16),
            pltpu.VMEM((27, C, LANES), F32),
            pltpu.VMEM((27, C, C), F32),
            dma((3,)),
            dma((3,)),
        ],
        compiler_params=pltpu.CompilerParams(vmem_limit_bytes=60 * 1024 * 1024),
    )(*results)


def solution(mesh):
    assert mesh.shape["gx"] == 16 and mesh.shape["gy"] == 8
    placed = (
        P(None, "gx", "gy", None),
        P(None, "gx", "gy", None),
        P(),
        P("gx", "gy"),
        P("gx", "gy"),
    )
    return jax.shard_map(
        shards,
        mesh=mesh,
        in_specs=placed,
        out_specs=(P(None, "gx", "gy", None), P(None, "gx", "gy", None), P()),
        check_vma=False,
    )
```

time: 65.7 us -> 53.2 us (0.81)
  Pallas kernels: 60.1 us -> 52.4 us
  local copies, waits for them, and re-layouts: 4.7 us -> 0 us
    pallas_call x1, Pallas kernels: 60.1 us -> 49.6 us  [shards(): pl.pallas_call(body, out_shape=(block, block, jax.ShapeDtypeStruct((27, C...]
    unnamed x5 -> x0, local copies, waits for them, and re-layouts: 4.7 us -> none
    pallas_call x0 -> x1, Pallas kernels: none -> 2.77 us  [shards(): pl.pallas_call(hand_on, out_shape=shapes, in_specs=[hbm] * 3, out_specs=(...]
where the time goes in v2:
time: 53.2 us; the launch traced here: 53 us
  Pallas kernels  52.4 us (98%)
  between operations  0.64 us (1%)
    pallas_call x1, Pallas kernels, shards(): pl.pallas_call(body, out_shape=(block, block, jax.ShapeDtypeStruct((27, C...  49.6 us
    pallas_call x1, Pallas kernels, shards(): pl.pallas_call(hand_on, out_shape=shapes, in_specs=[hbm] * 3, out_specs=(...  2.77 us

profile of v2, /device:TPU:1, one launch (start us, length us, event | category | flops | bytes accessed | tf_op | source)
XLA Modules:
  0.0 53.0 jit_solution(12541180859949980711)
XLA Ops:
  0.6 49.6 %shard_map.76 = (bf16[96,2,8,128]{3,2,1,0:T(8,128)(2,1)}, bf16[96,2,8,128]{3,2,1,0:T(8,128)(2,1)}, f32[27,96,128]{2,1,0:T(8,128)}) custom-call(bf16[96,2,8,128]{3,2,1,0:T(8,128)(2,1)} %refs_0_.1, bf16[96,2,8,128]{3,2,1,0:T(8,128)(2,1)} %refs_1_.1, bf16[27,96,96]{2,1,0:T(8,128)(2,1)} %refs_2_.1, s32[2,8]{1,0:T(2,128)} %refs_3_.1, s32[2,8]{1,0:T(2,128)} %refs_4_.1), custom_call_target="tpu_custom_call" | custom-call | flops 3057647616 | bytes 4194304 | tf_op jit(solution)/shard_map/pallas_call | solution.py:395
  50.2 2.8 %shard_map.77 = (bf16[96,2,8,128]{3,2,1,0:T(8,128)(2,1)}, bf16[96,2,8,128]{3,2,1,0:T(8,128)(2,1)}, f32[27,96,96]{2,1,0:T(8,128)}) custom-call(bf16[96,2,8,128]{3,2,1,0:T(8,128)(2,1)} %get-tuple-element.6.a, bf16[96,2,8,128]{3,2,1,0:T(8,128)(2,1)} %get-tuple-element.7.b, f32[27,96,128]{2,1,0:T(8,128)} %get-tuple-element.8.c), custom_call_target="tpu_custom_call" | custom-call | tf_op jit(solution)/shard_map/pallas_call | solution.py:438

commit v3 on v2

v3 whole, which is shorter than its diff:
```python
import math

import jax
import jax.numpy as jnp
from jax import lax
from jax.experimental import pallas as pl
from jax.experimental.pallas import tpu as pltpu
from jax.sharding import PartitionSpec as P

MESH = pl.DeviceIdType.MESH
F32 = jnp.float32
BF16 = jnp.bfloat16
C = 96
NX, NY, NZ = 2, 8, 128
OWNERS = 14
BLOCK = 84
NEAR, FAR, SAME = 0, 1, 2
NT = (((1,), (1,)), ((), ()))


def kernel(
    scale,
    feat_hbm, cot_hbm, w_hbm, ground, thick,
    out, grad_in, full,
    feat, cot, w, pf, pc, tmp, shifted, lf, lb, red, core_box, late_box, mid_box, late_ring, mid_ring, tout,
    load_sem, halo_send, halo_recv, core_send, core_recv,
    rs_send, rs_recv, ag_send, ag_recv, ring_send, ring_recv, plane_sem,
):
    gx = lax.axis_index("gx")
    gy = lax.axis_index("gy")
    core = lax.rem(gx, 2)
    cx = lax.div(gx, 4)
    cy = lax.rem(lax.div(gx, 2), 2) * 2 + lax.rem(gy, 2)
    cz = lax.div(gy, 2)
    near_gx = gx + 1 - 2 * core
    far_gx = gx - 1 + 2 * core
    has_far = jnp.logical_and(far_gx >= 0, far_gx < 16)
    near_x = 1 - core
    far_x = core
    near_a = 2 * (1 - core)
    far_a = 2 * core

    loads = [
        pltpu.make_async_copy(feat_hbm, feat, load_sem.at[0]),
        pltpu.make_async_copy(cot_hbm, cot, load_sem.at[1]),
        pltpu.make_async_copy(w_hbm, w, load_sem.at[2]),
    ]
    for load in loads:
        load.start()

    def chip(x, y, z):
        return (x * 4 + lax.div(y, 2) * 2 + core, z * 2 + lax.rem(y, 2))

    def step(dx, dy, dz):
        return lax.rem(cx + dx, 4), lax.rem(cy + dy, 4), lax.rem(cz + dz, 4)

    has_dy = {-1: gy > 0, 0: None, 1: gy < 7}

    def present(side, dy):
        terms = []
        if side == FAR:
            terms.append(has_far)
        if dy != 0:
            terms.append(has_dy[dy])
        if not terms:
            return None
        return terms[0] if len(terms) == 1 else jnp.logical_and(*terms)

    def when(cond, fn):
        if cond is None:
            fn()
        else:
            pl.when(cond)(fn)

    def halo_device(side, dy):
        return ({NEAR: near_gx, FAR: far_gx, SAME: gx}[side], gy + dy)

    halos = [(SAME, -1), (SAME, 1), (FAR, 0), (FAR, -1), (FAR, 1), (NEAR, 0)]
    rings = {
        "x": [chip(*step(d, 0, 0)) for d in (1, 2, 3)],
        "y": [chip(*step(0, d, 0)) for d in (1, 2, 3)],
        "z": [chip(*step(0, 0, d)) for d in (1, 2, 3)],
    }

    def signal(sem, device):
        pl.semaphore_signal(sem, inc=1, device_id=device, device_id_type=MESH)

    barrier = pltpu.get_barrier_semaphore()
    for side, dy in halos:
        when(present(side, dy), lambda side=side, dy=dy: signal(barrier, halo_device(side, dy)))
    for axis in "xyz":
        for device in rings[axis]:
            signal(barrier, device)

    rows = lax.broadcasted_iota(jnp.int32, (NY, NZ), 0)
    heights = lax.broadcasted_iota(jnp.int32, (NY, NZ), 1)

    def occupied(x):
        low = jnp.zeros((NY, NZ), jnp.int32)
        high = jnp.zeros((NY, NZ), jnp.int32)
        for y in range(NY):
            g = ground[x, y]
            low = jnp.where(rows == y, g, low)
            high = jnp.where(rows == y, g + thick[x, y], high)
        return jnp.logical_and(heights >= low, heights < high)

    def columns(src, dst, x, shifts):
        value = jnp.where(occupied(x)[None], src[:, x].astype(F32), 0.0)
        tmp[...] = value.reshape(C * NY, NZ)
        for y in range(NY):
            col = tmp[pl.ds(y, C, stride=NY), :]
            dst[x + 1, y + 1] = col.astype(BF16)
            if shifts:
                lanes = slice(y * NZ, (y + 1) * NZ)
                shifted[x, 0:C, lanes] = pltpu.roll(col, NZ - 1, 1).astype(BF16)
                shifted[x, C : 2 * C, lanes] = col.astype(BF16)
                shifted[x, 2 * C : 3 * C, lanes] = pltpu.roll(col, 1, 1).astype(BF16)

    loads[0].wait()
    for x in range(NX):
        columns(feat, pf, x, False)

    n_dy = jnp.where(gy > 0, 1, 0) + jnp.where(gy < 7, 1, 0)
    n_far = jnp.where(has_far, 1, 0)
    pl.semaphore_wait(barrier, n_dy + n_far * (n_dy + 1) + 1 + 9)

    src_y = {-1: 1, 0: 1, 1: NY}
    dst_y = {-1: NY + 1, 0: 1, 1: 0}
    len_y = {-1: 1, 0: NY, 1: 1}

    def halo_copy(which, side, dy):
        buf = (pf, pc)[which]
        n = len_y[dy]
        if side == SAME:
            src_x = dst_x = pl.ds(1, 2)
        elif side == NEAR:
            src_x, dst_x = pl.ds(2 - core, 1), pl.ds(3 * core, 1)
        else:
            src_x, dst_x = pl.ds(1 + core, 1), pl.ds(3 * (1 - core), 1)
        return pltpu.make_async_remote_copy(
            src_ref=buf.at[src_x, pl.ds(src_y[dy], n)],
            dst_ref=buf.at[dst_x, pl.ds(dst_y[dy], n)],
            send_sem=halo_send.at[which, side, dy + 1],
            recv_sem=halo_recv.at[which, side, dy + 1],
            device_id=halo_device(side, dy),
            device_id_type=MESH,
        )

    def send_halos(which):
        for side, dy in halos:
            when(present(side, dy), lambda side=side, dy=dy: halo_copy(which, side, dy).start())

    def recv_halos(which, sides):
        for side, dy in halos:
            if side in sides:
                when(present(side, -dy), lambda side=side, dy=dy: halo_copy(which, side, dy).wait_recv())

    def done_halos(which, sides):
        for side, dy in halos:
            if side in sides:
                when(present(side, dy), lambda side=side, dy=dy: halo_copy(which, side, dy).wait_send())

    def corner_copy(which, e):
        buf = (pf, pc)[which]
        y = pl.ds(0 if e < 0 else NY + 1, 1)
        return pltpu.make_async_remote_copy(
            src_ref=buf.at[pl.ds(2 - core, 1), y],
            dst_ref=buf.at[pl.ds(3 * core, 1), y],
            send_sem=halo_send.at[which, NEAR, e + 1],
            recv_sem=halo_recv.at[which, NEAR, e + 1],
            device_id=(near_gx, gy),
            device_id_type=MESH,
        )

    def corners(which, act):
        for e in (-1, 1):
            pl.when(has_dy[e])(lambda e=e: act(corner_copy(which, e)))

    def clear_edges(buf):
        zeros = jnp.zeros((C, NZ), BF16)

        def far_side():
            for y in range(NY + 2):
                buf[3 * core, y] = zeros

        def y_side(y):
            for x in range(NX + 2):
                buf[x, y] = zeros

        pl.when(jnp.logical_not(has_far))(far_side)
        pl.when(gy == 0)(lambda: y_side(0))
        pl.when(gy == 7)(lambda: y_side(NY + 1))

    send_halos(0)
    for device in rings["z"]:
        signal(plane_sem, device)
    loads[1].wait()
    for x in range(NX):
        columns(cot, pc, x, True)
    clear_edges(pf)
    clear_edges(pc)

    loads[2].wait()
    for c in range(3):
        lf[c * C : (c + 1) * C, :] = jnp.concatenate([w[ab * 3 + c] for ab in range(9)], axis=1)
        lb[c * C : (c + 1) * C, :] = jnp.concatenate(
            [w[26 - (ab * 3 + c)].T for ab in range(9)], axis=1
        )

    def weight_terms(xs, a):
        lhs = jnp.concatenate([shifted[x] for x in xs], axis=1)
        rhs = jnp.concatenate(
            [
                jnp.concatenate([pf[x + a, y + b] for x in xs for y in range(NY)], axis=1)
                for b in range(3)
            ],
            axis=0,
        )
        return lax.dot_general(lhs, rhs, NT, preferred_element_type=F32)

    def put(a, value, add):
        rest = jnp.concatenate([value[72 * q : 72 * q + 72, 256:288] for q in range(4)], axis=1)
        parts = (
            (0, 36, value[:, 0:128]), (36, 36, value[:, 128:256]), (72, 9, rest),
        )
        for start, n, part in parts:
            at = pl.ds(BLOCK * a + start, n)
            part = part.reshape(n, 8, 128)
            red[at] = red[at] + part if add else part
        if not add:
            red[pl.ds(BLOCK * a + 81, 3)] = jnp.zeros((3, 8, 128), F32)

    def core_copy(k, src, dst):
        return pltpu.make_async_remote_copy(
            src_ref=src, dst_ref=dst, send_sem=core_send.at[k], recv_sem=core_recv.at[k],
            device_id=(near_gx, gy), device_id_type=MESH,
        )

    def late_part(buf, m):
        return buf.at[pl.ds(2 * BLOCK * m, BLOCK)]

    def mid_part(buf, m):
        return buf.at[pl.ds(BLOCK + BLOCK // 2 * m, BLOCK // 2)]

    other = 1 - core
    recv_halos(0, (SAME,))
    corners(0, lambda copy: copy.start())
    put(1, weight_terms((near_x, far_x), 1), False)
    pairs = [core_copy(0, mid_part(red, other), core_box.at[pl.ds(BLOCK, BLOCK // 2)])]
    pairs[0].start()
    recv_halos(0, (NEAR,))
    corners(0, lambda copy: copy.wait_recv())
    put(near_a, weight_terms((near_x, far_x), near_a), False)
    pairs.append(core_copy(1, late_part(red, other), core_box.at[pl.ds(0, BLOCK)]))
    pairs[1].start()
    put(far_a, weight_terms((near_x,), far_a), False)

    def conv_pair(x, j, buf, lhs):
        stack = jnp.concatenate(
            [
                jnp.concatenate([buf[x + a, 2 * j + b], buf[x + a, 2 * j + b + 1]], axis=1)
                for a in range(3)
                for b in range(3)
            ],
            axis=0,
        )
        prod = jnp.dot(lhs[...], stack, preferred_element_type=F32)
        for half in range(2):
            part = prod[:, half * NZ : (half + 1) * NZ]
            col = (
                pltpu.roll(part[0:C], 1, 1) + part[C : 2 * C] + pltpu.roll(part[2 * C : 3 * C], NZ - 1, 1)
            )
            tout[pl.ds(2 * j + half, C, stride=NY), :] = col

    def conv(x, buf, lhs, dst):
        for j in range(NY // 2):
            conv_pair(x, j, buf, lhs)
        mask = occupied(x)
        dst[:, x] = jnp.where(mask[None], tout[...].reshape(C, NY, NZ), 0.0).astype(BF16)

    me = cx * 4 + cz
    plane = sorted(
        [(dx, dz) for dx in range(4) for dz in range(4) if (dx, dz) != (0, 0)],
        key=lambda d: -sum(min(v, 4 - v) for v in d),
    )

    def late_share(buf, j):
        return buf.at[pl.ds(2 * BLOCK * core + 6 * j, 6)]

    def mid_share(buf, j):
        return buf.at[pl.ds(BLOCK + BLOCK // 2 * core + 3 * j, 3)]

    shares = (mid_share, late_share)
    boxes = (mid_box, late_box)
    circles = (mid_ring, late_ring)

    def exchange(index):
        for dx, dz in plane:
            x, y, z = step(dx, 0, dz)
            j = x * 4 + z

            @pl.when(j < OWNERS)
            def _(device=chip(x, y, z), j=j, d=dx * 4 + dz):
                pltpu.make_async_remote_copy(
                    src_ref=shares[index](red, j), dst_ref=boxes[index].at[d],
                    send_sem=rs_send.at[index], recv_sem=rs_recv.at[index],
                    device_id=device, device_id_type=MESH,
                ).start()

    def drain(ref, sem):
        pltpu.make_async_copy(ref, ref, sem).wait()

    def owner(fn):
        pl.when(me < OWNERS)(fn)

    def collect(index):
        @owner
        def _():
            drain(boxes[index].at[pl.ds(1, 15)], rs_recv.at[index])
            circles[index][cy] = shares[index](red, me)[...] + jnp.sum(boxes[index][1:16], axis=0)
            for device in rings["y"]:
                here = circles[index].at[cy]
                pltpu.make_async_remote_copy(
                    src_ref=here, dst_ref=here, send_sem=ring_send.at[index], recv_sem=ring_recv.at[index],
                    device_id=device, device_id_type=MESH,
                ).start()

    def hand_out(index, j, device, d):
        share = shares[index](full, j)
        return pltpu.make_async_remote_copy(
            src_ref=share, dst_ref=share, send_sem=ag_send.at[index], recv_sem=ag_recv.at[index, d],
            device_id=device, device_id_type=MESH,
        )

    def pass_on(index, j):
        share = shares[index](full, j)
        core_copy(2 + index, share, share).start()

    def finish(index):
        @owner
        def _():
            drain(circles[index].at[pl.ds(0, 3)], ring_recv.at[index])
            terms = [circles[index][y] for y in range(4)]
            shares[index](full, me)[...] = ((terms[0] + terms[1]) + (terms[2] + terms[3])) * scale
            for dx, dz in plane:
                hand_out(index, me, chip(*step(dx, 0, dz)), dx * 4 + dz).start()
            pass_on(index, me)

    def gather(index):
        for dx, dz in reversed(plane):
            x, y, z = step(4 - dx, 0, 4 - dz)
            j = x * 4 + z

            @pl.when(j < OWNERS)
            def _(device=chip(x, y, z), j=j, d=dx * 4 + dz):
                hand_out(index, j, device, d).wait_recv()
                pass_on(index, j)

    pl.semaphore_wait(plane_sem, 3)
    for pair in pairs:
        pair.wait_recv()
    mid = mid_part(red, core)
    mid[...] = mid[...] + core_box[BLOCK : BLOCK + BLOCK // 2]
    exchange(0)
    late = late_part(red, core)
    late[...] = late[...] + core_box[0:BLOCK]
    recv_halos(0, (FAR,))
    put(far_a, weight_terms((far_x,), far_a), True)
    exchange(1)
    send_halos(1)
    conv(near_x, pf, lf, out)
    conv(far_x, pf, lf, out)
    collect(0)
    recv_halos(1, (SAME, NEAR))
    corners(1, lambda copy: copy.start())
    corners(1, lambda copy: copy.wait_recv())
    collect(1)
    conv(near_x, pc, lb, grad_in)
    finish(0)
    finish(1)
    gather(0)
    recv_halos(1, (FAR,))
    conv(far_x, pc, lb, grad_in)
    gather(1)
    for which in range(2):
        done_halos(which, (NEAR, SAME, FAR))
        corners(which, lambda copy: copy.wait_send())
    for copy in pairs:
        copy.wait_send()
    for index, box in enumerate(boxes):
        owner(lambda: drain(box.at[pl.ds(0, OWNERS - 1)], rs_send.at[index]))
        pl.when(me >= OWNERS)(lambda: drain(box.at[pl.ds(0, OWNERS)], rs_send.at[index]))
        owner(lambda: drain(circles[index].at[pl.ds(0, 3)], ring_send.at[index]))
        owner(lambda: drain(box.at[pl.ds(0, 15)], ag_send.at[index]))
    for index, part in enumerate((mid_part, late_part)):
        passed = part(full, other)
        core_copy(2 + index, passed, passed).wait()


def hand_on(a, b, c, x, y, z):
    x[...] = a[...]
    y[...] = b[...]
    for k in range(3):
        tiles = c[BLOCK * k : BLOCK * k + 81]
        left = tiles[0:36].reshape(3 * C, 128)
        right = tiles[36:72].reshape(3 * C, 128)
        rest = tiles[72:81].reshape(72, 128)
        rest = jnp.concatenate([rest[:, 32 * q : 32 * q + 32] for q in range(4)], axis=0)
        blocks = (
            left[:, 0:C],
            jnp.concatenate([left[:, C:128], right[:, 0:64]], axis=1),
            jnp.concatenate([right[:, 64:128], rest], axis=1),
        )
        for i, block in enumerate(blocks):
            z[9 * k + 3 * i : 9 * k + 3 * i + 3] = block.reshape(3, C, C)


def shards(features, cotangent, weights, ground, thick):
    voxels = NX * NY * NZ * lax.axis_size("gx") * lax.axis_size("gy")
    block = jax.ShapeDtypeStruct((C, NX, NY, NZ), BF16)
    hbm = pl.BlockSpec(memory_space=pltpu.HBM)
    vmem = pl.BlockSpec(memory_space=pltpu.VMEM)
    smem = pl.BlockSpec(memory_space=pltpu.SMEM)

    def body(*refs):
        kernel(1.0 / math.sqrt(voxels), *refs)

    dma = pltpu.SemaphoreType.DMA
    inner = pltpu.VMEM((C, NX, NY, NZ), BF16)
    results = pl.pallas_call(
        body,
        out_shape=(inner, inner, pltpu.VMEM((3 * BLOCK, 8, 128), F32)),
        in_specs=[hbm, hbm, hbm, smem, smem],
        out_specs=(vmem, vmem, vmem),
        scratch_shapes=[
            inner,
            inner,
            pltpu.VMEM((27, C, C), BF16),
            pltpu.VMEM((NX + 2, NY + 2, C, NZ), BF16),
            pltpu.VMEM((NX + 2, NY + 2, C, NZ), BF16),
            pltpu.VMEM((C * NY, NZ), F32),
            pltpu.VMEM((NX, 3 * C, NY * NZ), BF16),
            pltpu.VMEM((3 * C, 9 * C), BF16),
            pltpu.VMEM((3 * C, 9 * C), BF16),
            pltpu.VMEM((3 * BLOCK, 8, 128), F32),
            pltpu.VMEM((BLOCK + BLOCK // 2, 8, 128), F32),
            pltpu.VMEM((16, 6, 8, 128), F32),
            pltpu.VMEM((16, 3, 8, 128), F32),
            pltpu.VMEM((4, 6, 8, 128), F32),
            pltpu.VMEM((4, 3, 8, 128), F32),
            pltpu.VMEM((C * NY, NZ), F32),
            dma((3,)),
            dma((2, 3, 3)),
            dma((2, 3, 3)),
            dma((4,)),
            dma((4,)),
            dma((2,)),
            dma((2,)),
            dma((2,)),
            dma((2, 16)),
            dma((2,)),
            dma((2,)),
            pltpu.SemaphoreType.REGULAR,
        ],
        compiler_params=pltpu.CompilerParams(
            collective_id=0, has_side_effects=True, vmem_limit_bytes=48 * 1024 * 1024
        ),
        cost_estimate=pl.CostEstimate(
            flops=3 * 2 * NX * NY * NZ * 27 * C * C, bytes_accessed=4 * 2**20, transcendentals=0
        ),
    )(*[pltpu.with_memory_space_constraint(v, pltpu.HBM) for v in (features, cotangent, weights, ground, thick)])
    return pl.pallas_call(
        hand_on,
        out_shape=(block, block, jax.ShapeDtypeStruct((27, C, C), F32)),
        in_specs=[vmem] * 3,
        out_specs=(vmem,) * 3,
        compiler_params=pltpu.CompilerParams(vmem_limit_bytes=16 * 1024 * 1024),
    )(*results)


def solution(mesh):
    assert mesh.shape["gx"] == 16 and mesh.shape["gy"] == 8
    placed = (
        P(None, "gx", "gy", None),
        P(None, "gx", "gy", None),
        P(),
        P("gx", "gy"),
        P("gx", "gy"),
    )
    return jax.shard_map(
        shards,
        mesh=mesh,
        in_specs=placed,
        out_specs=(P(None, "gx", "gy", None), P(None, "gx", "gy", None), P()),
        check_vma=False,
    )
```

time: 53.2 us -> 43.5 us (0.82)
  Pallas kernels: 52.4 us -> 42.7 us
    pallas_call x2, Pallas kernels: 52.4 us -> 42.7 us  [the longest x1 40.9 us: shards(): pl.pallas_call(body, out_shape=(inner, inner, pltpu.VMEM((3 * BLOCK, 8, 1...]
where the time goes in v3:
time: 43.5 us; the launch traced here: 43.3 us
  Pallas kernels  42.7 us (98%)
  between operations  0.64 us (1%)
    pallas_call x1, Pallas kernels, shards(): pl.pallas_call(body, out_shape=(inner, inner, pltpu.VMEM((3 * BLOCK, 8, 1...  40.9 us
    pallas_call x1, Pallas kernels, shards(): pl.pallas_call(hand_on, out_shape=(block, block, jax.ShapeDtypeStruct((27...  1.85 us

profile of v3, /device:TPU:1, one launch (start us, length us, event | category | flops | bytes accessed | tf_op | source)
XLA Modules:
  0.0 43.3 jit_solution(16620351134462327331)
XLA Ops:
  0.6 40.9 %shard_map.76 = (bf16[96,2,8,128]{3,2,1,0:T(8,128)(2,1)S(1)}, bf16[96,2,8,128]{3,2,1,0:T(8,128)(2,1)S(1)}, f32[252,8,128]{2,1,0:T(8,128)S(1)}) custom-call(bf16[96,2,8,128]{3,2,1,0:T(8,128)(2,1)} %refs_0_.1, bf16[96,2,8,128]{3,2,1,0:T(8,128)(2,1)} %refs_1_.1, bf16[27,96,96]{2,1,0:T(8,128)(2,1)} %refs_2_.1, s32[2,8]{1,0:T(2,128)} %refs_3_.1, s32[2,8]{1,0:T(2,128)} %refs_4_.1), custom_call_target="tpu_custom_call" | custom-call | flops 3057647616 | bytes 4194304 | tf_op jit(solution)/shard_map/pallas_call | solution.py:430
  41.5 1.8 %shard_map.77 = (bf16[96,2,8,128]{3,2,1,0:T(8,128)(2,1)}, bf16[96,2,8,128]{3,2,1,0:T(8,128)(2,1)}, f32[27,96,96]{2,1,0:T(8,128)}) custom-call(bf16[96,2,8,128]{3,2,1,0:T(8,128)(2,1)S(1)} %get-tuple-element.6.a, bf16[96,2,8,128]{3,2,1,0:T(8,128)(2,1)S(1)} %get-tuple-element.7.b, f32[252,8,128]{2,1,0:T(8,128)S(1)} %get-tuple-element.8.c), custom_call_target="tpu_custom_call" | custom-call | tf_op jit(solution)/shard_map/pallas_call | solution.py:472

commit v4 on v3

--- a/solution.py
+++ b/solution.py
@@ -146,9 +146,10 @@
             device_id_type=MESH,
         )
 
-    def send_halos(which):
+    def send_halos(which, sides=(SAME, FAR, NEAR)):
         for side, dy in halos:
-            when(present(side, dy), lambda side=side, dy=dy: halo_copy(which, side, dy).start())
+            if side in sides:
+                when(present(side, dy), lambda side=side, dy=dy: halo_copy(which, side, dy).start())
 
     def recv_halos(which, sides):
         for side, dy in halos:
@@ -197,23 +198,12 @@
     loads[1].wait()
     for x in range(NX):
         columns(cot, pc, x, True)
-    clear_edges(pf)
-    clear_edges(pc)
-
-    loads[2].wait()
-    for c in range(3):
-        lf[c * C : (c + 1) * C, :] = jnp.concatenate([w[ab * 3 + c] for ab in range(9)], axis=1)
-        lb[c * C : (c + 1) * C, :] = jnp.concatenate(
-            [w[26 - (ab * 3 + c)].T for ab in range(9)], axis=1
-        )
-
-    def weight_terms(xs, a):
-        lhs = jnp.concatenate([shifted[x] for x in xs], axis=1)
+    send_halos(1, (SAME, NEAR))
+
+    def weight_terms(xs, a, ys):
+        lhs = jnp.concatenate([shifted[x, :, y * NZ : (y + 1) * NZ] for x in xs for y in ys], axis=1)
         rhs = jnp.concatenate(
-            [
-                jnp.concatenate([pf[x + a, y + b] for x in xs for y in range(NY)], axis=1)
-                for b in range(3)
-            ],
+            [jnp.concatenate([pf[x + a, y + b] for x in xs for y in ys], axis=1) for b in range(3)],
             axis=0,
         )
         return lax.dot_general(lhs, rhs, NT, preferred_element_type=F32)
@@ -243,17 +233,23 @@
         return buf.at[pl.ds(BLOCK + BLOCK // 2 * m, BLOCK // 2)]
 
     other = 1 - core
+    inner, outer, both = range(1, NY - 1), (0, NY - 1), (near_x, far_x)
+    put(1, weight_terms(both, 1, inner), False)
+    put(far_a, weight_terms((near_x,), far_a, inner), False)
+    clear_edges(pf)
+    clear_edges(pc)
+    recv_halos(0, (NEAR,))
+    put(near_a, weight_terms(both, near_a, inner), False)
     recv_halos(0, (SAME,))
     corners(0, lambda copy: copy.start())
-    put(1, weight_terms((near_x, far_x), 1), False)
+    put(1, weight_terms(both, 1, outer), True)
     pairs = [core_copy(0, mid_part(red, other), core_box.at[pl.ds(BLOCK, BLOCK // 2)])]
     pairs[0].start()
-    recv_halos(0, (NEAR,))
+    put(far_a, weight_terms((near_x,), far_a, outer), True)
     corners(0, lambda copy: copy.wait_recv())
-    put(near_a, weight_terms((near_x, far_x), near_a), False)
+    put(near_a, weight_terms(both, near_a, outer), True)
     pairs.append(core_copy(1, late_part(red, other), core_box.at[pl.ds(0, BLOCK)]))
     pairs[1].start()
-    put(far_a, weight_terms((near_x,), far_a), False)
 
     def conv_pair(x, j, buf, lhs):
         stack = jnp.concatenate(
@@ -357,30 +353,36 @@
                 pass_on(index, j)
 
     pl.semaphore_wait(plane_sem, 3)
-    for pair in pairs:
-        pair.wait_recv()
+    pairs[0].wait_recv()
     mid = mid_part(red, core)
     mid[...] = mid[...] + core_box[BLOCK : BLOCK + BLOCK // 2]
     exchange(0)
+    pairs[1].wait_recv()
     late = late_part(red, core)
     late[...] = late[...] + core_box[0:BLOCK]
     recv_halos(0, (FAR,))
-    put(far_a, weight_terms((far_x,), far_a), True)
+    send_halos(1, (FAR,))
+    put(far_a, weight_terms((far_x,), far_a, range(NY)), True)
     exchange(1)
-    send_halos(1)
+    loads[2].wait()
+    for c in range(3):
+        lf[c * C : (c + 1) * C, :] = jnp.concatenate([w[ab * 3 + c] for ab in range(9)], axis=1)
+        lb[c * C : (c + 1) * C, :] = jnp.concatenate(
+            [w[26 - (ab * 3 + c)].T for ab in range(9)], axis=1
+        )
     conv(near_x, pf, lf, out)
+    collect(0)
     conv(far_x, pf, lf, out)
-    collect(0)
     recv_halos(1, (SAME, NEAR))
     corners(1, lambda copy: copy.start())
+    collect(1)
+    finish(0)
     corners(1, lambda copy: copy.wait_recv())
-    collect(1)
     conv(near_x, pc, lb, grad_in)
-    finish(0)
     finish(1)
-    gather(0)
     recv_halos(1, (FAR,))
     conv(far_x, pc, lb, grad_in)
+    gather(0)
     gather(1)
     for which in range(2):
         done_halos(which, (NEAR, SAME, FAR))
@@ -397,9 +399,13 @@
         core_copy(2 + index, passed, passed).wait()
 
 
-def hand_on(a, b, c, x, y, z):
-    x[...] = a[...]
-    y[...] = b[...]
+def hand_on(a, b, c, x, y, z, unpacked, sem):
+    copies = [
+        pltpu.make_async_copy(a, x, sem.at[3]),
+        pltpu.make_async_copy(b, y, sem.at[4]),
+    ]
+    for copy in copies:
+        copy.start()
     for k in range(3):
         tiles = c[BLOCK * k : BLOCK * k + 81]
         left = tiles[0:36].reshape(3 * C, 128)
@@ -412,7 +418,12 @@
             jnp.concatenate([right[:, 64:128], rest], axis=1),
         )
         for i, block in enumerate(blocks):
-            z[9 * k + 3 * i : 9 * k + 3 * i + 3] = block.reshape(3, C, C)
+            unpacked[9 * k + 3 * i : 9 * k + 3 * i + 3] = block.reshape(3, C, C)
+        part = pl.ds(9 * k, 9)
+        copies.append(pltpu.make_async_copy(unpacked.at[part], z.at[part], sem.at[k]))
+        copies[-1].start()
+    for copy in copies:
+        copy.wait()
 
 
 def shards(features, cotangent, weights, ground, thick):
@@ -473,7 +484,8 @@
         hand_on,
         out_shape=(block, block, jax.ShapeDtypeStruct((27, C, C), F32)),
         in_specs=[vmem] * 3,
-        out_specs=(vmem,) * 3,
+        out_specs=(hbm,) * 3,
+        scratch_shapes=[pltpu.VMEM((27, C, C), F32), dma((5,))],
         compiler_params=pltpu.CompilerParams(vmem_limit_bytes=16 * 1024 * 1024),
     )(*results)
 

time: 43.5 us -> 41.2 us (0.947)
  Pallas kernels: 42.7 us -> 40.4 us
    pallas_call x1, Pallas kernels: 40.9 us -> 39 us  [shards(): pl.pallas_call(body, out_shape=(inner, inner, pltpu.VMEM((3 * BLOCK, 8, 1...]
    pallas_call x1, Pallas kernels: 1.85 us -> 1.39 us  [shards(): pl.pallas_call(hand_on, out_shape=(block, block, jax.ShapeDtypeStruct((27...]
where the time goes in v4:
time: 41.2 us; the launch traced here: 41 us
  Pallas kernels  40.4 us (98%)
  between operations  0.64 us (2%)
    pallas_call x1, Pallas kernels, shards(): pl.pallas_call(body, out_shape=(inner, inner, pltpu.VMEM((3 * BLOCK, 8, 1...  39 us
    pallas_call x1, Pallas kernels, shards(): pl.pallas_call(hand_on, out_shape=(block, block, jax.ShapeDtypeStruct((27...  1.39 us

profile of v4, /device:TPU:1, one launch (start us, length us, event | category | flops | bytes accessed | tf_op | source)
XLA Modules:
  0.0 41.0 jit_solution(11765621589745237078)
XLA Ops:
  0.6 39.0 %shard_map.76 = (bf16[96,2,8,128]{3,2,1,0:T(8,128)(2,1)S(1)}, bf16[96,2,8,128]{3,2,1,0:T(8,128)(2,1)S(1)}, f32[252,8,128]{2,1,0:T(8,128)S(1)}) custom-call(bf16[96,2,8,128]{3,2,1,0:T(8,128)(2,1)} %refs_0_.1, bf16[96,2,8,128]{3,2,1,0:T(8,128)(2,1)} %refs_1_.1, bf16[27,96,96]{2,1,0:T(8,128)(2,1)} %refs_2_.1, s32[2,8]{1,0:T(2,128)} %refs_3_.1, s32[2,8]{1,0:T(2,128)} %refs_4_.1), custom_call_target="tpu_custom_call" | custom-call | flops 3057647616 | bytes 4194304 | tf_op jit(solution)/shard_map/pallas_call | solution.py:441
  39.6 1.4 %shard_map.77 = (bf16[96,2,8,128]{3,2,1,0:T(8,128)(2,1)}, bf16[96,2,8,128]{3,2,1,0:T(8,128)(2,1)}, f32[27,96,96]{2,1,0:T(8,128)}) custom-call(bf16[96,2,8,128]{3,2,1,0:T(8,128)(2,1)S(1)} %get-tuple-element.6.a, bf16[96,2,8,128]{3,2,1,0:T(8,128)(2,1)S(1)} %get-tuple-element.7.b, f32[252,8,128]{2,1,0:T(8,128)S(1)} %get-tuple-element.8.c), custom_call_target="tpu_custom_call" | custom-call | tf_op jit(solution)/shard_map/pallas_call | solution.py:483

commit v5 on v4

--- a/solution.py
+++ b/solution.py
@@ -14,15 +14,16 @@
 NX, NY, NZ = 2, 8, 128
 OWNERS = 14
 BLOCK = 84
+STREAM = 42
 NEAR, FAR, SAME = 0, 1, 2
 NT = (((1,), (1,)), ((), ()))
 
 
 def kernel(
     scale,
-    feat_hbm, cot_hbm, w_hbm, ground, thick,
+    feat_hbm, cot_hbm, w_hbm, ground_hbm, thick_hbm,
     out, grad_in, full,
-    feat, cot, w, pf, pc, tmp, shifted, lf, lb, red, core_box, late_box, mid_box, late_ring, mid_ring, tout,
+    feat, cot, w, ground, thick, pf, pc, tmp, shifted, lf, lb, red, core_box, box, ring, tout,
     load_sem, halo_send, halo_recv, core_send, core_recv,
     rs_send, rs_recv, ag_send, ag_recv, ring_send, ring_recv, plane_sem,
 ):
@@ -44,6 +45,8 @@
         pltpu.make_async_copy(feat_hbm, feat, load_sem.at[0]),
         pltpu.make_async_copy(cot_hbm, cot, load_sem.at[1]),
         pltpu.make_async_copy(w_hbm, w, load_sem.at[2]),
+        pltpu.make_async_copy(ground_hbm, ground, load_sem.at[3]),
+        pltpu.make_async_copy(thick_hbm, thick, load_sem.at[4]),
     ]
     for load in loads:
         load.start()
@@ -116,6 +119,8 @@
                 shifted[x, C : 2 * C, lanes] = col.astype(BF16)
                 shifted[x, 2 * C : 3 * C, lanes] = pltpu.roll(col, 1, 1).astype(BF16)
 
+    loads[3].wait()
+    loads[4].wait()
     loads[0].wait()
     for x in range(NX):
         columns(feat, pf, x, False)
@@ -230,7 +235,7 @@
         return buf.at[pl.ds(2 * BLOCK * m, BLOCK)]
 
     def mid_part(buf, m):
-        return buf.at[pl.ds(BLOCK + BLOCK // 2 * m, BLOCK // 2)]
+        return buf.at[pl.ds(BLOCK + STREAM * m, STREAM)]
 
     other = 1 - core
     inner, outer, both = range(1, NY - 1), (0, NY - 1), (near_x, far_x)
@@ -243,7 +248,7 @@
     recv_halos(0, (SAME,))
     corners(0, lambda copy: copy.start())
     put(1, weight_terms(both, 1, outer), True)
-    pairs = [core_copy(0, mid_part(red, other), core_box.at[pl.ds(BLOCK, BLOCK // 2)])]
+    pairs = [core_copy(0, mid_part(red, other), core_box.at[pl.ds(BLOCK, STREAM)])]
     pairs[0].start()
     put(far_a, weight_terms((near_x,), far_a, outer), True)
     corners(0, lambda copy: copy.wait_recv())
@@ -280,15 +285,12 @@
         key=lambda d: -sum(min(v, 4 - v) for v in d),
     )
 
-    def late_share(buf, j):
-        return buf.at[pl.ds(2 * BLOCK * core + 6 * j, 6)]
-
-    def mid_share(buf, j):
-        return buf.at[pl.ds(BLOCK + BLOCK // 2 * core + 3 * j, 3)]
-
-    shares = (mid_share, late_share)
-    boxes = (mid_box, late_box)
-    circles = (mid_ring, late_ring)
+    def stream(base):
+        return lambda buf, j: buf.at[pl.ds(base + 3 * j, 3)]
+
+    shares = [stream(BLOCK + STREAM * core), stream(2 * BLOCK * core), stream(2 * BLOCK * core + STREAM)]
+    boxes = [box.at[i] for i in range(3)]
+    circles = [ring.at[i] for i in range(3)]
 
     def exchange(index):
         for dx, dz in plane:
@@ -330,7 +332,7 @@
 
     def pass_on(index, j):
         share = shares[index](full, j)
-        core_copy(2 + index, share, share).start()
+        core_copy(min(2 + index, 3), share, share).start()
 
     def finish(index):
         @owner
@@ -355,7 +357,7 @@
     pl.semaphore_wait(plane_sem, 3)
     pairs[0].wait_recv()
     mid = mid_part(red, core)
-    mid[...] = mid[...] + core_box[BLOCK : BLOCK + BLOCK // 2]
+    mid[...] = mid[...] + core_box[BLOCK : BLOCK + STREAM]
     exchange(0)
     pairs[1].wait_recv()
     late = late_part(red, core)
@@ -364,6 +366,7 @@
     send_halos(1, (FAR,))
     put(far_a, weight_terms((far_x,), far_a, range(NY)), True)
     exchange(1)
+    exchange(2)
     loads[2].wait()
     for c in range(3):
         lf[c * C : (c + 1) * C, :] = jnp.concatenate([w[ab * 3 + c] for ab in range(9)], axis=1)
@@ -376,24 +379,27 @@
     recv_halos(1, (SAME, NEAR))
     corners(1, lambda copy: copy.start())
     collect(1)
+    collect(2)
     finish(0)
     corners(1, lambda copy: copy.wait_recv())
     conv(near_x, pc, lb, grad_in)
     finish(1)
+    finish(2)
+    gather(0)
     recv_halos(1, (FAR,))
     conv(far_x, pc, lb, grad_in)
-    gather(0)
     gather(1)
+    gather(2)
     for which in range(2):
         done_halos(which, (NEAR, SAME, FAR))
         corners(which, lambda copy: copy.wait_send())
     for copy in pairs:
         copy.wait_send()
-    for index, box in enumerate(boxes):
-        owner(lambda: drain(box.at[pl.ds(0, OWNERS - 1)], rs_send.at[index]))
-        pl.when(me >= OWNERS)(lambda: drain(box.at[pl.ds(0, OWNERS)], rs_send.at[index]))
+    for index, slots in enumerate(boxes):
+        owner(lambda: drain(slots.at[pl.ds(0, OWNERS - 1)], rs_send.at[index]))
+        pl.when(me >= OWNERS)(lambda: drain(slots.at[pl.ds(0, OWNERS)], rs_send.at[index]))
         owner(lambda: drain(circles[index].at[pl.ds(0, 3)], ring_send.at[index]))
-        owner(lambda: drain(box.at[pl.ds(0, 15)], ag_send.at[index]))
+        owner(lambda: drain(slots.at[pl.ds(0, 15)], ag_send.at[index]))
     for index, part in enumerate((mid_part, late_part)):
         passed = part(full, other)
         core_copy(2 + index, passed, passed).wait()
@@ -431,7 +437,6 @@
     block = jax.ShapeDtypeStruct((C, NX, NY, NZ), BF16)
     hbm = pl.BlockSpec(memory_space=pltpu.HBM)
     vmem = pl.BlockSpec(memory_space=pltpu.VMEM)
-    smem = pl.BlockSpec(memory_space=pltpu.SMEM)
 
     def body(*refs):
         kernel(1.0 / math.sqrt(voxels), *refs)
@@ -441,12 +446,14 @@
     results = pl.pallas_call(
         body,
         out_shape=(inner, inner, pltpu.VMEM((3 * BLOCK, 8, 128), F32)),
-        in_specs=[hbm, hbm, hbm, smem, smem],
+        in_specs=[hbm] * 5,
         out_specs=(vmem, vmem, vmem),
         scratch_shapes=[
             inner,
             inner,
             pltpu.VMEM((27, C, C), BF16),
+            pltpu.SMEM((NX, NY), jnp.int32),
+            pltpu.SMEM((NX, NY), jnp.int32),
             pltpu.VMEM((NX + 2, NY + 2, C, NZ), BF16),
             pltpu.VMEM((NX + 2, NY + 2, C, NZ), BF16),
             pltpu.VMEM((C * NY, NZ), F32),
@@ -454,23 +461,21 @@
             pltpu.VMEM((3 * C, 9 * C), BF16),
             pltpu.VMEM((3 * C, 9 * C), BF16),
             pltpu.VMEM((3 * BLOCK, 8, 128), F32),
-            pltpu.VMEM((BLOCK + BLOCK // 2, 8, 128), F32),
-            pltpu.VMEM((16, 6, 8, 128), F32),
-            pltpu.VMEM((16, 3, 8, 128), F32),
-            pltpu.VMEM((4, 6, 8, 128), F32),
-            pltpu.VMEM((4, 3, 8, 128), F32),
+            pltpu.VMEM((BLOCK + STREAM, 8, 128), F32),
+            pltpu.VMEM((3, 16, 3, 8, 128), F32),
+            pltpu.VMEM((3, 4, 3, 8, 128), F32),
             pltpu.VMEM((C * NY, NZ), F32),
-            dma((3,)),
+            dma((5,)),
             dma((2, 3, 3)),
             dma((2, 3, 3)),
             dma((4,)),
             dma((4,)),
-            dma((2,)),
-            dma((2,)),
-            dma((2,)),
-            dma((2, 16)),
-            dma((2,)),
-            dma((2,)),
+            dma((3,)),
+            dma((3,)),
+            dma((3,)),
+            dma((3, 16)),
+            dma((3,)),
+            dma((3,)),
             pltpu.SemaphoreType.REGULAR,
         ],
         compiler_params=pltpu.CompilerParams(

time: 41.2 us -> 39.8 us (0.966)
  Pallas kernels: 40.4 us -> 39 us
    pallas_call x1, Pallas kernels: 39 us -> 37.6 us  [shards(): pl.pallas_call(body, out_shape=(inner, inner, pltpu.VMEM((3 * BLOCK, 8, 1...]
where the time goes in v5:
time: 39.8 us; the launch traced here: 39.6 us
  Pallas kernels  39 us (98%)
  between operations  0.64 us (2%)
    pallas_call x1, Pallas kernels, shards(): pl.pallas_call(body, out_shape=(inner, inner, pltpu.VMEM((3 * BLOCK, 8, 1...  37.6 us
    pallas_call x1, Pallas kernels, shards(): pl.pallas_call(hand_on, out_shape=(block, block, jax.ShapeDtypeStruct((27...  1.39 us

profile of v5, /device:TPU:1, one launch (start us, length us, event | category | flops | bytes accessed | tf_op | source)
XLA Modules:
  0.0 39.6 jit_solution(2051034140084493410)
XLA Ops:
  0.6 37.6 %shard_map.76 = (bf16[96,2,8,128]{3,2,1,0:T(8,128)(2,1)S(1)}, bf16[96,2,8,128]{3,2,1,0:T(8,128)(2,1)S(1)}, f32[252,8,128]{2,1,0:T(8,128)S(1)}) custom-call(bf16[96,2,8,128]{3,2,1,0:T(8,128)(2,1)} %refs_0_.1, bf16[96,2,8,128]{3,2,1,0:T(8,128)(2,1)} %refs_1_.1, bf16[27,96,96]{2,1,0:T(8,128)(2,1)} %refs_2_.1, s32[2,8]{1,0:T(2,128)} %refs_3_.1, s32[2,8]{1,0:T(2,128)} %refs_4_.1), custom_call_target="tpu_custom_call" | custom-call | flops 3057647616 | bytes 4194304 | tf_op jit(solution)/shard_map/pallas_call | solution.py:446
  38.3 1.4 %shard_map.77 = (bf16[96,2,8,128]{3,2,1,0:T(8,128)(2,1)}, bf16[96,2,8,128]{3,2,1,0:T(8,128)(2,1)}, f32[27,96,96]{2,1,0:T(8,128)}) custom-call(bf16[96,2,8,128]{3,2,1,0:T(8,128)(2,1)S(1)} %get-tuple-element.6.a, bf16[96,2,8,128]{3,2,1,0:T(8,128)(2,1)S(1)} %get-tuple-element.7.b, f32[252,8,128]{2,1,0:T(8,128)S(1)} %get-tuple-element.8.c), custom_call_target="tpu_custom_call" | custom-call | tf_op jit(solution)/shard_map/pallas_call | solution.py:488

commit v6 on v5

--- a/solution.py
+++ b/solution.py
@@ -23,7 +23,7 @@
     scale,
     feat_hbm, cot_hbm, w_hbm, ground_hbm, thick_hbm,
     out, grad_in, full,
-    feat, cot, w, ground, thick, pf, pc, tmp, shifted, lf, lb, red, core_box, box, ring, tout,
+    feat, cot, w, ground, thick, pf, pc, tmp, shifted, lf, lb, red, core_box, mid_box, late_box, mid_ring, late_ring, tout,
     load_sem, halo_send, halo_recv, core_send, core_recv,
     rs_send, rs_recv, ag_send, ag_recv, ring_send, ring_recv, plane_sem,
 ):
@@ -285,12 +285,13 @@
         key=lambda d: -sum(min(v, 4 - v) for v in d),
     )
 
-    def stream(base):
-        return lambda buf, j: buf.at[pl.ds(base + 3 * j, 3)]
-
-    shares = [stream(BLOCK + STREAM * core), stream(2 * BLOCK * core), stream(2 * BLOCK * core + STREAM)]
-    boxes = [box.at[i] for i in range(3)]
-    circles = [ring.at[i] for i in range(3)]
+    def stream(base, n):
+        return lambda buf, j: buf.at[pl.ds(base + n * j, n)]
+
+    shares = [stream(BLOCK + STREAM * core, 3)]
+    shares += [stream(2 * BLOCK * core + 2 * OWNERS * i, 2) for i in range(3)]
+    boxes = [mid_box] + [late_box.at[i] for i in range(3)]
+    circles = [mid_ring] + [late_ring.at[i] for i in range(3)]
 
     def exchange(index):
         for dx, dz in plane:
@@ -367,6 +368,8 @@
     put(far_a, weight_terms((far_x,), far_a, range(NY)), True)
     exchange(1)
     exchange(2)
+    exchange(3)
+    collect(0)
     loads[2].wait()
     for c in range(3):
         lf[c * C : (c + 1) * C, :] = jnp.concatenate([w[ab * 3 + c] for ab in range(9)], axis=1)
@@ -374,22 +377,24 @@
             [w[26 - (ab * 3 + c)].T for ab in range(9)], axis=1
         )
     conv(near_x, pf, lf, out)
-    collect(0)
     conv(far_x, pf, lf, out)
     recv_halos(1, (SAME, NEAR))
     corners(1, lambda copy: copy.start())
     collect(1)
     collect(2)
+    collect(3)
     finish(0)
     corners(1, lambda copy: copy.wait_recv())
     conv(near_x, pc, lb, grad_in)
     finish(1)
     finish(2)
+    finish(3)
     gather(0)
     recv_halos(1, (FAR,))
     conv(far_x, pc, lb, grad_in)
     gather(1)
     gather(2)
+    gather(3)
     for which in range(2):
         done_halos(which, (NEAR, SAME, FAR))
         corners(which, lambda copy: copy.wait_send())
@@ -462,20 +467,22 @@
             pltpu.VMEM((3 * C, 9 * C), BF16),
             pltpu.VMEM((3 * BLOCK, 8, 128), F32),
             pltpu.VMEM((BLOCK + STREAM, 8, 128), F32),
-            pltpu.VMEM((3, 16, 3, 8, 128), F32),
-            pltpu.VMEM((3, 4, 3, 8, 128), F32),
+            pltpu.VMEM((16, 3, 8, 128), F32),
+            pltpu.VMEM((3, 16, 2, 8, 128), F32),
+            pltpu.VMEM((4, 3, 8, 128), F32),
+            pltpu.VMEM((3, 4, 2, 8, 128), F32),
             pltpu.VMEM((C * NY, NZ), F32),
             dma((5,)),
             dma((2, 3, 3)),
             dma((2, 3, 3)),
             dma((4,)),
             dma((4,)),
-            dma((3,)),
-            dma((3,)),
-            dma((3,)),
-            dma((3, 16)),
-            dma((3,)),
-            dma((3,)),
+            dma((4,)),
+            dma((4,)),
+            dma((4,)),
+            dma((4, 16)),
+            dma((4,)),
+            dma((4,)),
             pltpu.SemaphoreType.REGULAR,
         ],
         compiler_params=pltpu.CompilerParams(

time: 39.8 us -> 39.7 us (level)
  no operation moved by 1% of the time
where the time goes in v6:
time: 39.7 us; the launch traced here: 39.6 us
  Pallas kernels  38.9 us (98%)
  between operations  0.64 us (2%)
    pallas_call x1, Pallas kernels, shards(): pl.pallas_call(body, out_shape=(inner, inner, pltpu.VMEM((3 * BLOCK, 8, 1...  37.6 us
    pallas_call x1, Pallas kernels, shards(): pl.pallas_call(hand_on, out_shape=(block, block, jax.ShapeDtypeStruct((27...  1.39 us

profile of v6, /device:TPU:1, one launch (start us, length us, event | category | flops | bytes accessed | tf_op | source)
XLA Modules:
  0.0 39.6 jit_solution(1022504315708503427)
XLA Ops:
  0.6 37.6 %shard_map.76 = (bf16[96,2,8,128]{3,2,1,0:T(8,128)(2,1)S(1)}, bf16[96,2,8,128]{3,2,1,0:T(8,128)(2,1)S(1)}, f32[252,8,128]{2,1,0:T(8,128)S(1)}) custom-call(bf16[96,2,8,128]{3,2,1,0:T(8,128)(2,1)} %refs_0_.1, bf16[96,2,8,128]{3,2,1,0:T(8,128)(2,1)} %refs_1_.1, bf16[27,96,96]{2,1,0:T(8,128)(2,1)} %refs_2_.1, s32[2,8]{1,0:T(2,128)} %refs_3_.1, s32[2,8]{1,0:T(2,128)} %refs_4_.1), custom_call_target="tpu_custom_call" | custom-call | flops 3057647616 | bytes 4194304 | tf_op jit(solution)/shard_map/pallas_call | solution.py:451
  38.2 1.4 %shard_map.77 = (bf16[96,2,8,128]{3,2,1,0:T(8,128)(2,1)}, bf16[96,2,8,128]{3,2,1,0:T(8,128)(2,1)}, f32[27,96,96]{2,1,0:T(8,128)}) custom-call(bf16[96,2,8,128]{3,2,1,0:T(8,128)(2,1)S(1)} %get-tuple-element.6.a, bf16[96,2,8,128]{3,2,1,0:T(8,128)(2,1)S(1)} %get-tuple-element.7.b, f32[252,8,128]{2,1,0:T(8,128)S(1)} %get-tuple-element.8.c), custom_call_target="tpu_custom_call" | custom-call | tf_op jit(solution)/shard_map/pallas_call | solution.py:495

commit v7 on v6

--- a/solution.py
+++ b/solution.py
@@ -205,13 +205,13 @@
         columns(cot, pc, x, True)
     send_halos(1, (SAME, NEAR))
 
-    def weight_terms(xs, a, ys):
+    def weight_terms(xs, a, ys, cut=slice(None)):
         lhs = jnp.concatenate([shifted[x, :, y * NZ : (y + 1) * NZ] for x in xs for y in ys], axis=1)
         rhs = jnp.concatenate(
             [jnp.concatenate([pf[x + a, y + b] for x in xs for y in ys], axis=1) for b in range(3)],
             axis=0,
         )
-        return lax.dot_general(lhs, rhs, NT, preferred_element_type=F32)
+        return lax.dot_general(lhs, rhs[cut], NT, preferred_element_type=F32)
 
     def put(a, value, add):
         rest = jnp.concatenate([value[72 * q : 72 * q + 72, 256:288] for q in range(4)], axis=1)
@@ -365,8 +365,16 @@
     late[...] = late[...] + core_box[0:BLOCK]
     recv_halos(0, (FAR,))
     send_halos(1, (FAR,))
-    put(far_a, weight_terms((far_x,), far_a, range(NY)), True)
+    head = weight_terms((far_x,), far_a, range(NY), slice(0, 128))
+    at = pl.ds(BLOCK * far_a, 36)
+    red[at] = red[at] + head.reshape(36, 8, 128)
     exchange(1)
+    tail = weight_terms((far_x,), far_a, range(NY), slice(128, 288))
+    rest = jnp.concatenate([tail[72 * q : 72 * q + 72, 128:160] for q in range(4)], axis=1)
+    at = pl.ds(BLOCK * far_a + 36, 36)
+    red[at] = red[at] + tail[:, 0:128].reshape(36, 8, 128)
+    at = pl.ds(BLOCK * far_a + 72, 9)
+    red[at] = red[at] + rest.reshape(9, 8, 128)
     exchange(2)
     exchange(3)
     collect(0)

time: 39.7 us -> 39.5 us (level)
  no operation moved by 1% of the time
where the time goes in v7:
time: 39.5 us; the launch traced here: 39.4 us
  Pallas kernels  38.8 us (98%)
  between operations  0.64 us (2%)
    pallas_call x1, Pallas kernels, shards(): pl.pallas_call(body, out_shape=(inner, inner, pltpu.VMEM((3 * BLOCK, 8, 1...  37.4 us
    pallas_call x1, Pallas kernels, shards(): pl.pallas_call(hand_on, out_shape=(block, block, jax.ShapeDtypeStruct((27...  1.39 us

profile of v7, /device:TPU:1, one launch (start us, length us, event | category | flops | bytes accessed | tf_op | source)
XLA Modules:
  0.0 39.4 jit_solution(11737264115258623571)
XLA Ops:
  0.6 37.4 %shard_map.76 = (bf16[96,2,8,128]{3,2,1,0:T(8,128)(2,1)S(1)}, bf16[96,2,8,128]{3,2,1,0:T(8,128)(2,1)S(1)}, f32[252,8,128]{2,1,0:T(8,128)S(1)}) custom-call(bf16[96,2,8,128]{3,2,1,0:T(8,128)(2,1)} %refs_0_.1, bf16[96,2,8,128]{3,2,1,0:T(8,128)(2,1)} %refs_1_.1, bf16[27,96,96]{2,1,0:T(8,128)(2,1)} %refs_2_.1, s32[2,8]{1,0:T(2,128)} %refs_3_.1, s32[2,8]{1,0:T(2,128)} %refs_4_.1), custom_call_target="tpu_custom_call" | custom-call | flops 3057647616 | bytes 4194304 | tf_op jit(solution)/shard_map/pallas_call | solution.py:459
  38.0 1.4 %shard_map.77 = (bf16[96,2,8,128]{3,2,1,0:T(8,128)(2,1)}, bf16[96,2,8,128]{3,2,1,0:T(8,128)(2,1)}, f32[27,96,96]{2,1,0:T(8,128)}) custom-call(bf16[96,2,8,128]{3,2,1,0:T(8,128)(2,1)S(1)} %get-tuple-element.6.a, bf16[96,2,8,128]{3,2,1,0:T(8,128)(2,1)S(1)} %get-tuple-element.7.b, f32[252,8,128]{2,1,0:T(8,128)S(1)} %get-tuple-element.8.c), custom_call_target="tpu_custom_call" | custom-call | tf_op jit(solution)/shard_map/pallas_call | solution.py:503
